TPU v7x, 256 devices: a whole 4x4x8 slice. The times are simulated.
256 devices in a mesh: angle: 2 (over z_hi), src: 16 (over x, z_lo), tile: 8 (over y, core).
Axes of the slice: x: 4, y: 4, z: 8 (z_hi: 2, z_lo: 4; z = z_hi * 4 + z_lo), core: 2. Of those that a mesh axis runs over, the one named last changes fastest.
Arguments:
- spectra: bfloat16 [32, 16, 2, 4096], P('tile', 'angle', None, 'src'), may hold values from -6 to 6
- cotangent: float32 [32, 128, 128], P('tile'), may hold values from -6 to 6
- pupil_field: bfloat16 [2048, 2, 4096], P(('angle', 'src', 'tile')), may hold values from -4 to 4
- source_grid: int32 [2048, 2], P(('angle', 'src')), may hold values from -8 to 8
- cutoff: int32 [2048], P(('angle', 'src')), may hold values from 256 to 784
- stencil: int32 [2048, 4], P(('angle', 'src')), may hold values from 0 to 15, as said below
- interp_weights: bfloat16 [2048, 4], P(('angle', 'src')), may hold values from 0.099609375 to 1
- source_weight: float32 [2048], P(('angle', 'src')), may hold values from 0.5 to 4
Outputs:
- grad_spectra: float32 [32, 16, 2, 4096], P('tile', 'angle', None, 'src')
Inputs may be any that keep to these rules, and one draw needn't show every extreme that they name: `stencil`: the four entries of each source point are the corners c, c + 1, c + 4, c + 5 of one cell of the 16 reference angles laid out as a 4 x 4 grid (c = 4 i + j with i, j below 3).
All inputs are finite; a program needn't handle non-finite values.
Results may differ from a plain program's by a relative error of at most 0.0074.
Values may be sent and summed in bfloat16 or wider, within the bound.
A program may use at most 64 MiB of HBM per device.

v0:
```python
import math

import jax
import jax.numpy as jnp
from jax import lax
from jax.sharding import PartitionSpec as P

FQ = 64
NP = 128
ANGLES = 16


highest = lax.Precision.HIGHEST


def dft_tables(side_orders, samples):
    frequency = jnp.arange(side_orders, dtype=jnp.int32) - side_orders // 2
    position = jnp.arange(samples, dtype=jnp.int32)
    residue = jnp.mod(position[:, None] * frequency[None, :], samples)
    phases = residue.astype(jnp.float32) * (2.0 * math.pi / samples)
    factor = 1.0 / math.sqrt(side_orders)
    cosine = jnp.cos(phases) * factor
    sine_table = jnp.sin(phases) * factor
    right_table = jnp.stack(
        [jnp.stack([cosine.T, sine_table.T], axis=1), jnp.stack([-sine_table.T, cosine.T], axis=1)],
        axis=0,
    )
    left_table = jnp.stack(
        [jnp.stack([cosine, -sine_table], axis=1), jnp.stack([sine_table, cosine], axis=1)], axis=0
    )
    return (right_table.astype(jnp.bfloat16), left_table.astype(jnp.bfloat16))


def angle_weights(stencil, interp_weights, angle_count):
    labels = jnp.arange(angle_count, dtype=jnp.int32)
    matches = (stencil[:, :, None] == labels[None, None, :]).astype(jnp.float32)
    return jnp.sum(matches * interp_weights.astype(jnp.float32)[:, :, None], axis=1).astype(
        jnp.bfloat16
    )


def pupil_disc(source_grid, cutoff, side_orders):
    frequency = jnp.arange(side_orders, dtype=jnp.int32) - side_orders // 2
    along_first = frequency[None, :, None] + source_grid[:, 0][:, None, None]
    along_second = frequency[None, None, :] + source_grid[:, 1][:, None, None]
    within = along_first * along_first + along_second * along_second <= cutoff[:, None, None]
    return within.astype(jnp.float32).reshape(source_grid.shape[0], side_orders * side_orders)


def gradient_block(mixed, pupil_rows, disc, weight, cotangent, right_table, left_table):
    number = mixed.shape[0]
    tile_count = mixed.shape[1]
    side_orders = right_table.shape[1]
    pupil_real = pupil_rows[:, 0].astype(jnp.float32)[:, None, :]
    pupil_imag = pupil_rows[:, 1].astype(jnp.float32)[:, None, :]
    inside = disc[:, None, :]
    mixed_real = mixed[:, :, 0]
    mixed_imag = mixed[:, :, 1]
    field_real = inside * (pupil_real * mixed_real - pupil_imag * mixed_imag)
    field_imag = inside * (pupil_real * mixed_imag + pupil_imag * mixed_real)
    spectrum = jnp.stack([field_real, field_imag], axis=2).astype(jnp.bfloat16)
    spectrum = spectrum.reshape(number, tile_count, 2, side_orders, side_orders)
    halfway = jnp.einsum(
        "btpyf,pfqx->btyqx", spectrum, right_table, preferred_element_type=jnp.float32
    ).astype(jnp.bfloat16)
    image_field = jnp.einsum(
        "ryqf,btfqx->btryx", left_table, halfway, preferred_element_type=jnp.float32
    )
    factor = weight[:, None, None, None] * cotangent[None]
    adjoint = (factor[:, :, None] * image_field).astype(jnp.bfloat16)
    back_half = jnp.einsum(
        "btryx,rxqf->btyqf", adjoint, left_table, preferred_element_type=jnp.float32
    ).astype(jnp.bfloat16)
    spectral = jnp.einsum(
        "pfqy,btyqx->btpfx", right_table, back_half, preferred_element_type=jnp.float32
    )
    spectral = spectral.reshape(number, tile_count, 2, side_orders * side_orders)
    back_real = spectral[:, :, 0]
    back_imag = spectral[:, :, 1]
    grad_real = inside * (pupil_real * back_real + pupil_imag * back_imag)
    grad_imag = inside * (pupil_real * back_imag - pupil_imag * back_real)
    return jnp.stack([grad_real, grad_imag], axis=2)


def shards(
    spectra, cotangent, pupil_field, source_grid, cutoff, stencil, interp_weights, source_weight
):
    tile_count = spectra.shape[0]
    angle_local = spectra.shape[1]
    angle_groups = lax.axis_size("angle")
    row_groups = lax.axis_size("src")
    local_sources = source_grid.shape[0]
    total_sources = local_sources * angle_groups * row_groups
    orders = FQ * FQ
    slice_orders = orders // row_groups
    right_table, left_table = dft_tables(FQ, NP)
    weights = angle_weights(stencil, interp_weights, ANGLES)
    disc = pupil_disc(source_grid, cutoff, FQ)
    scaled = source_weight * (2.0 / math.sqrt(total_sources))
    gathered = lax.all_gather(spectra, "src", axis=3, tiled=True)
    every_angle = lax.all_gather(gathered, "angle", axis=1, tiled=True)
    mixed = jnp.einsum("sk,tkpf->stpf", weights, every_angle, preferred_element_type=jnp.float32)
    pieces = lax.all_gather(pupil_field, "tile", axis=0, tiled=True)
    amount = pieces.shape[0]
    block_size = math.gcd(amount, 4)
    rounds = amount // block_size

    def one_block(parts):
        block_pupil, block_mixed, block_disc, block_scaled = parts
        return gradient_block(
            block_mixed, block_pupil, block_disc, block_scaled, cotangent, right_table, left_table
        )

    stacked = lax.map(
        one_block,
        (
            pieces.reshape(rounds, block_size, 2, orders),
            mixed.reshape(rounds, block_size, tile_count, 2, orders),
            disc.reshape(rounds, block_size, orders),
            scaled.reshape(rounds, block_size),
        ),
    )
    gradient = stacked.reshape(amount, tile_count, 2, row_groups, slice_orders)
    wide_weights = weights.astype(jnp.float32).reshape(amount, angle_groups, angle_local)
    added = jnp.einsum("sak,stpgf->takpgf", wide_weights, gradient, precision=highest)
    added = added.reshape(tile_count, ANGLES, 2, orders)
    by_rows = lax.psum_scatter(added, "src", scatter_dimension=3, tiled=True)
    result = lax.psum_scatter(by_rows, "angle", scatter_dimension=1, tiled=True)
    return result


def solution(mesh):
    placed = (
        P("tile", "angle", None, "src"),
        P("tile", None, None),
        P(("angle", "src", "tile"), None, None),
        P(("angle", "src"), None),
        P(("angle", "src")),
        P(("angle", "src"), None),
        P(("angle", "src"), None),
        P(("angle", "src")),
    )
    return jax.shard_map(
        shards,
        mesh=mesh,
        in_specs=placed,
        out_specs=P("tile", "angle", None, "src"),
        check_vma=False,
    )
```

profile of v0, /device:TPU:16, one launch (start us, length us, event | category | flops | bytes accessed | tf_op | source)
XLA Modules:
  0.0 425.7 jit_solution(3677264045082080651)
XLA Ops:
  7.3 50.7 %all_gather.10 = bf16[4,8,2,4096]{3,1,2,0:T(8,128)(2,1)} all-gather(bf16[4,8,2,256]{3,1,2,0:T(8,128)(2,1)S(1)} %copy.45), channel_id=1, replica_groups=mesh['angle'=2,'src'=16,'tile'=8] {'src'}, dimensions={3}, use_global_device_ids=true | all-gather | bytes 557056 | tf_op jit(solution)/shard_map/all_gather | solution.py:100
  62.9 1.1 copy.48
  65.7 1.4 compare_convert_fusion
  67.0 30.9 %all-gather.5.cloned.1.call-done = bf16[4,16,2,4096]{3,1,2,0:T(8,128)(2,1)} async-done(((bf16[4,8,2,4096]{3,1,2,0:T(8,128)(2,1)}), bf16[4,16,2,4096]{3,1,2,0:T(8,128)(2,1)}) %all-gather.5.cloned.1.call-update) | async-done | bytes 1048592 | tf_op jit(solution)/shard_map/all_gather | solution.py:101
  97.9 2.5 fusion.39
  100.4 7.8 %copy.74 = f32[64,4,2,4096]{3,2,1,0:T(2,128)} copy(f32[64,4,2,4096]{3,0,2,1:T(8,128)S(1)} %fusion.39) | data formatting | bytes 16777216 | tf_op jit(solution)/shard_map/while | solution.py:114
  108.2 12.4 %all-gather.3.cloned.1.call-done = bf16[64,2,4096]{2,1,0:T(2,128)(2,1)} async-done(((bf16[8,2,4096]{2,1,0:T(2,128)(2,1)}), bf16[64,2,4096]{2,1,0:T(2,128)(2,1)}) %all-gather.3.cloned.1.call-update) | async-done | bytes 1048592 | tf_op jit(solution)/shard_map/all_gather | solution.py:103
  120.6 159.0 %while.10 = (s32[]{:T(128)}, f32[16,4,4,2,4096]{4,3,2,1,0:T(2,128)}, f32[16,4,4096]{2,1,0:T(4,128)}, bf16[16,4,2,4096]{3,2,1,0:T(2,128)(2,1)}, f32[16,4]{1,0:T(8...) while((s32[]{:T(128)}, ...), condition=%wide.region_2.3_spmd, body=%wide.region_1.2_spmd.sunk | while | flops 406355968 | bytes 12976805 | solution.py:114
  122.4 1.1 dynamic-slice_bitcast_fusion.4
  123.5 2.0 convert_reduce_fusion.3
  129.2 1.3 fusion.69
  132.4 1.1 dynamic-slice_bitcast_fusion.4
  133.5 2.0 convert_reduce_fusion.3
  139.2 1.3 fusion.69
  142.3 1.1 dynamic-slice_bitcast_fusion.4
  143.4 2.0 convert_reduce_fusion.3
  149.2 1.3 fusion.69
  150.4 0.9 constant_dynamic-slice_fusion.3
  152.3 1.1 dynamic-slice_bitcast_fusion.4
  153.3 2.0 convert_reduce_fusion.3
  159.1 1.3 fusion.69
  162.2 1.1 dynamic-slice_bitcast_fusion.4
  163.3 2.0 convert_reduce_fusion.3
  169.0 1.3 fusion.69
  172.1 1.1 dynamic-slice_bitcast_fusion.4
  173.2 2.0 convert_reduce_fusion.3
  179.0 1.3 fusion.69
  182.1 1.1 dynamic-slice_bitcast_fusion.4
  183.1 2.0 convert_reduce_fusion.3
  188.9 1.3 fusion.69
  192.0 1.1 dynamic-slice_bitcast_fusion.4
  193.1 2.0 convert_reduce_fusion.3
  198.8 1.3 fusion.69
  201.9 1.1 dynamic-slice_bitcast_fusion.4
  203.0 2.0 convert_reduce_fusion.3
  208.7 1.3 fusion.69
  211.9 1.1 dynamic-slice_bitcast_fusion.4
  213.0 2.0 convert_reduce_fusion.3
  218.7 1.3 fusion.69
  221.8 1.1 dynamic-slice_bitcast_fusion.4
  222.9 2.0 convert_reduce_fusion.3
  228.7 1.3 fusion.69
  231.8 1.1 dynamic-slice_bitcast_fusion.4
  232.8 2.0 convert_reduce_fusion.3
  238.6 1.3 fusion.69
  241.7 1.1 dynamic-slice_bitcast_fusion.4
  242.7 2.0 convert_reduce_fusion.3
  248.5 1.3 fusion.69
  251.6 1.1 dynamic-slice_bitcast_fusion.4
  252.7 2.0 convert_reduce_fusion.3
  258.4 1.3 fusion.69
  261.5 1.1 dynamic-slice_bitcast_fusion.4
  262.6 2.0 convert_reduce_fusion.3
  268.3 1.3 fusion.69
  271.4 1.1 dynamic-slice_bitcast_fusion.4
  272.5 2.0 convert_reduce_fusion.3
  278.3 1.3 fusion.69
  279.6 11.8 %reshape.380 = f32[64,4,2,16,256]{4,3,2,1,0:T(8,128)} reshape(f32[16,4,4,2,4096]{4,3,2,1,0:T(2,128)} %get-tuple-element.52) | data formatting | bytes 16777216 | tf_op jit(solution)/shard_map/reshape | solution.py:123
  291.4 10.6 %fusion.21 = f32[4,2,8,2,16,256]{5,2,1,4,3,0:T(8,128)S(1)} fusion(f32[64,4,2,16,256,1]{4,3,2,1,0,5:T(8,128)} %bitcast.181, bf16[64,16]{0,1:T(8,128)(2,1)S(1)} %select_reduce_fusion), kind=kOutput, calls=%fused_computation.37 | convolution fusion | flops 402653184 | bytes 10487808 | tf_op jit(solution)/shard_map/sak,stpgf->takpgf/dot_general | solution.py:125
  302.0 1.2 copy.51
  303.2 1.6 reshape.381
  304.9 93.5 %reduce-scatter.3.cloned.1.call-done = f32[4,16,2,256]{3,1,2,0:T(8,128)} async-done(((f32[4,16,2,4096]{3,1,2,0:T(8,128)}), f32[4,16,2,256]{3,1,2,0:T(8,128)}) %reduce-scatter.3.cloned.1.call-update) | async-done | bytes 131088 | tf_op jit(solution)/shard_map/reduce_scatter | solution.py:127
  398.4 19.3 %reduce-scatter.5.cloned.1.call-done = f32[4,8,2,256]{3,1,2,0:T(8,128)} async-done(((f32[4,16,2,256]{3,1,2,0:T(8,128)}), f32[4,8,2,256]{3,1,2,0:T(8,128)}) %reduce-scatter.5.cloned.1.call-update) | async-done | bytes 65552 | tf_op jit(solution)/shard_map/reduce_scatter | solution.py:128
  417.6 1.5 copy.52
  (249 shorter events, 94.7 us)
Async XLA Ops:
  6.5 91.4 %all-gather.5.cloned.1.call-start = ((), (), s32[]{:S(2)}) async-start(), calls=%async_computation.3 | async-start | bytes 1572864 | tf_op jit(solution)/shard_map/all_gather | solution.py:101
  58.1 62.5 %all-gather.3.cloned.1.call-start = ((), (), s32[]{:S(2)}) async-start(), calls=%async_computation.2 | async-start | bytes 1179648 | tf_op jit(solution)/shard_map/all_gather | solution.py:103
  58.8 339.5 %reduce-scatter.3.cloned.1.call-start = ((), (), s32[]{:S(2)}) async-start(), calls=%async_computation.4 | async-start | bytes 2228224 | tf_op jit(solution)/shard_map/reduce_scatter | solution.py:127
  304.8 112.8 %reduce-scatter.5.cloned.1.call-start = ((), (), s32[]{:S(2)}) async-start(), calls=%async_computation.5 | async-start | bytes 196608 | tf_op jit(solution)/shard_map/reduce_scatter | solution.py:128
Sparse Core Ops, SparseCore 0:
  58.2 39.6 all-gather.4
  99.8 20.7 all-gather.2
  304.9 93.3 reduce-scatter.2
  400.7 16.9 reduce-scatter.4
where the time goes:
time: 430 us; the launch traced here: 426 us
  waiting for transfers between devices  157 us (37%)
  local copies, waits for them, and re-layouts  96.3 us (22%)
  other arithmetic  70.1 us (16%)
  blocking collectives  50.7 us (12%)
  matrix products  36.9 us (9%)
  between operations  13.2 us (3%)
    reduce_scatter x1, waiting for transfers between devices, shards(): by_rows = lax.psum_scatter(added, 'src', scatter_dimension=3, tiled=True)  93.5 us
    all_gather x1, blocking collectives, shards(): gathered = lax.all_gather(spectra, 'src', axis=3, tiled=True)  50.7 us
    another operation x18, other arithmetic  31.7 us
    all_gather x1, waiting for transfers between devices, shards(): every_angle = lax.all_gather(gathered, 'angle', axis=1, tiled=True)  30.9 us
    dynamic_update_slice x16, other arithmetic, shards(): lax.map(one_block, (pieces.reshape(rounds, block_size, 2, orders), mixed....  20.6 us
    reduce_scatter x1, waiting for transfers between devices, shards(): result = lax.psum_scatter(by_rows, 'angle', scatter_dimension=1, tiled=True)  19.3 us
    squeeze x16, local copies, waits for them, and re-layouts, shards(): lax.map(one_block, (pieces.reshape(rounds, block_size, 2, orders), mixed....  17.2 us
    dynamic_slice x32, local copies, waits for them, and re-layouts, shards(): lax.map(one_block, (pieces.reshape(rounds, block_size, 2, orders), mixed....  15 us
  transfers between devices with their start and end apart: 4, of which 4 were waited for; matrix products, arithmetic and copies ran while one was open for 4% of the time, Pallas kernels for 0%

commit v1 on v0

v1 whole, which is shorter than its diff:
```python
import functools
import math

import jax
import jax.numpy as jnp
import ml_dtypes
import numpy as np
from jax import lax
from jax.experimental import pallas as pl
from jax.experimental.pallas import tpu as pltpu
from jax.sharding import PartitionSpec as P

FQ = 64
NP = 128
NX, NY, NZ = 4, 4, 8
BF = jnp.bfloat16
F32 = jnp.float32
MESH = pl.DeviceIdType.MESH


def dft_matrices():
    f = np.arange(FQ) - FQ // 2
    phase = np.mod(np.arange(NP)[:, None] * f[None, :], NP) * (2 * math.pi / NP)
    c, s = np.cos(phase) / math.sqrt(FQ), np.sin(phase) / math.sqrt(FQ)
    right = np.zeros((2, 2, 64, 2, 2, 128))
    left = np.zeros((2, 128, 2, 2, 32))
    for p in range(2):
        right[0, p, :, p, 0], right[0, p, :, p, 1] = c.T, s.T
        right[1, p, :, p, 0], right[1, p, :, p, 1] = -s.T, c.T
        left[0, :, p, 0], left[0, :, p, 1] = c[:, p::2], -s[:, p::2]
        left[1, :, p, 0], left[1, :, p, 1] = s[:, p::2], c[:, p::2]
    right, left = right.reshape(256, 512), left.reshape(256, 128)
    return [np.ascontiguousarray(v).astype(ml_dtypes.bfloat16) for v in (right, left, left.T, right.T)]


def dot(a, b):
    return jnp.dot(a, b, preferred_element_type=F32)


def columns_of(shape, dim):
    c = lax.broadcasted_iota(jnp.int32, shape, dim)
    x, z, k8, i2 = c >> 7, (c >> 4) & 7, (c >> 1) & 7, c & 1
    return (z >> 2) * 8 + k8, 2 * (x * 4 + (z & 3)) + i2


def source_block(n, e, spec, pupil, right, left, left_t, right_t, cot):
    mixed = dot(e, spec)
    mr, mi = mixed[:, :128], mixed[:, 128:]
    pr, pi = pupil[:, :128].astype(F32), pupil[:, 128:].astype(F32)
    field = jnp.concatenate([(pr * mr - pi * mi).astype(BF), (pr * mi + pi * mr).astype(BF)], axis=1)
    half = dot(field, right).astype(BF)
    wide = jnp.concatenate([cot, cot], axis=1)
    wide = jnp.concatenate([wide, wide], axis=0)
    rows = []
    for q in range(n // 2):
        pair = []
        for s in (2 * q, 2 * q + 1):
            pair.append(jnp.concatenate([half[s * 32 : s * 32 + 32, c * 128 : c * 128 + 128] for c in range(4)], axis=0))
        image = dot(left, jnp.concatenate(pair, axis=1))
        adjoint = (image * wide).astype(BF)
        back = dot(left_t, adjoint).astype(BF)
        for s in range(2):
            rows.append(jnp.concatenate([back[c * 32 : c * 32 + 32, s * 128 : s * 128 + 128] for c in range(4)], axis=1))
    spectrum = dot(jnp.concatenate(rows, axis=0), right_t)
    br, bi = spectrum[:, :128], spectrum[:, 128:]
    return jnp.concatenate([(pr * br + pi * bi).astype(BF), (pr * bi - pi * br).astype(BF)], axis=1)


def kernel(
    own_spec, own_pupil, cot, stencil, interp, weight, grid, cutoff, right, left, left_t, right_t,
    out,
    spec, pupil, mixrow, e, et, acc, send_x, recv_x, send_z, recv_z,
    zs_sem, zr_sem, xs_sem, xr_sem, ps_sem, pr_sem, cs_sem, cr_sem, rxs_sem, rxr_sem, rzs_sem, rzr_sem,
):
    angle, src, tile = lax.axis_index("angle"), lax.axis_index("src"), lax.axis_index("tile")
    x, z = src // 4, angle * 4 + lax.rem(src, 4)
    y, core = tile // 2, lax.rem(tile, 2)

    def at_x(d):
        return {"src": lax.rem(x + d, NX) * 4 + lax.rem(src, 4)}

    def at_z(d):
        w = lax.rem(z + d, NZ)
        return {"angle": w // 4, "src": x * 4 + lax.rem(w, 4)}

    def at_y(d):
        return {"tile": lax.rem(y + d, NY) * 2 + core}

    twin = {"tile": y * 2 + 1 - core}
    peers = [at_z(d) for d in range(1, NZ)] + [at_x(d) for d in range(1, NX)] + [at_y(d) for d in range(1, NY)] + [twin]
    barrier = pltpu.get_barrier_semaphore()
    for peer in peers:
        pl.semaphore_signal(barrier, inc=1, device_id=peer, device_id_type=MESH)
    pl.semaphore_wait(barrier, len(peers))

    def remote(src_ref, dst_ref, send, recv, peer):
        return pltpu.make_async_remote_copy(
            src_ref=src_ref, dst_ref=dst_ref, send_sem=send, recv_sem=recv, device_id=peer, device_id_type=MESH
        )

    zrows = pl.ds(pl.multiple_of(x * 128 + z * 16, 16), 16)
    xrows = pl.ds(pl.multiple_of(x * 128, 128), 128)

    def gather_z(t, d):
        rows = spec.at[t, zrows, :]
        return remote(own_spec.at[t], rows, zs_sem.at[t, d - 1], zr_sem.at[t, d - 1], at_z(d))

    def gather_x(t, d):
        rows = spec.at[t, xrows, :]
        return remote(rows, rows, xs_sem.at[t, d - 1], xr_sem.at[t, d - 1], at_x(d))

    for t in range(4):
        for d in range(1, NZ):
            gather_z(t, d).start()
    for t in range(4):
        spec[t, zrows, :] = own_spec[t]

    lane = lax.broadcasted_iota(jnp.int32, (32, 128), 1)
    fa = 2 * lax.broadcasted_iota(jnp.int32, (32, 128), 0) + (lane >> 6) - 32
    fb = (lane & 63) - 32

    def mask(s8, carry):
        s = tile * 8 + s8
        da, db = fa + grid[s, 0], fb + grid[s, 1]
        inside = da * da + db * db <= cutoff[s]
        inside = jnp.concatenate([inside, inside], axis=1)
        rows = pl.ds(pl.multiple_of(s * 32, 32), 32)
        value = own_pupil[pl.ds(pl.multiple_of(s8 * 32, 32), 32), :].astype(F32)
        pupil[rows, :] = jnp.where(inside, value, 0.0).astype(BF)
        return carry

    lax.fori_loop(0, 8, mask, 0)

    def pupil_rows(yy):
        return pupil.at[pl.ds(pl.multiple_of((yy * 2 + core) * 256, 256), 256), :]

    def pupil_y(d):
        return remote(pupil_rows(y), pupil_rows(y), ps_sem.at[d - 1], pr_sem.at[d - 1], at_y(d))

    def pupil_core(j):
        rows = pupil_rows(lax.rem(y + j, NY))
        return remote(rows, rows, cs_sem.at[j], cr_sem.at[j], twin)

    for d in range(1, NY):
        pupil_y(d).start()
    pupil_core(0).start()

    ks, _ = columns_of((64, 512), 1)
    mix = jnp.zeros((64, 512), F32)
    for j in range(4):
        mix += jnp.where(stencil[:, j : j + 1] == ks, interp[:, j : j + 1].astype(F32), 0.0)
    mixrow[...] = mix
    _, i_row = columns_of((32, 512), 1)
    diagonal = (lax.broadcasted_iota(jnp.int32, (32, 512), 0) == i_row).astype(F32)

    def fill_e(s, carry):
        row = mixrow[pl.ds(s, 1), :]
        e[pl.ds(pl.multiple_of(s * 32, 32), 32), :] = (row * diagonal).astype(BF)
        return carry

    lax.fori_loop(0, 64, fill_e, 0)
    scaled = (mix * (weight[...] * (2.0 / math.sqrt(2048)))).T.astype(BF)
    _, i_col = columns_of((512, 512), 0)
    spread = lax.broadcasted_iota(jnp.int32, (512, 512), 1)
    hit = (spread & 31) == i_col
    source_of = lax.broadcasted_iota(jnp.int32, (64, 512), 1) >> 5
    source_at = lax.broadcasted_iota(jnp.int32, (64, 512), 0)
    for yy in range(4):
        pick = (source_of + yy * 16 == source_at).astype(BF)
        et[yy] = jnp.where(hit, dot(scaled, pick), 0.0).astype(BF)

    for t in range(4):
        for d in range(1, NZ):
            gather_z(t, d).wait_recv()
        for d in range(1, NX):
            gather_x(t, d).start()

    def reduce_x(t, d):
        to = lax.rem(x + d, NX)
        rows = send_x.at[t, pl.ds(pl.multiple_of(to * 128, 128), 128), :]
        return remote(rows, recv_x.at[t, d - 1], rxs_sem.at[t, d - 1], rxr_sem.at[t, d - 1], at_x(d))

    def reduce_z(t, d):
        to = lax.rem(z + d, NZ)
        rows = send_z.at[t, pl.ds(pl.multiple_of(to * 16, 16), 16), :]
        return remote(rows, recv_z.at[t, d - 1], rzs_sem.at[t, d - 1], rzr_sem.at[t, d - 1], at_z(d))

    def turn_x(t):
        total = send_x[t, xrows, :].astype(F32)
        for d in range(1, NX):
            reduce_x(t, d).wait_recv()
        for d in range(1, NX):
            total += recv_x[t, d - 1].astype(F32)
        send_z[t] = total.astype(BF)
        for d in range(1, NZ):
            reduce_z(t, d).start()

    def turn_z(t):
        total = send_z[t, pl.ds(pl.multiple_of(z * 16, 16), 16), :].astype(F32)
        for d in range(1, NZ):
            reduce_z(t, d).wait_recv()
        for d in range(1, NZ):
            total += recv_z[t, d - 1].astype(F32)
        out[t] = total

    def one_tile(t, carry):
        for d in range(1, NX):
            gather_x(t, d).wait_recv()

        def one_block(j, inner):
            yy = lax.rem(y + j, NY)

            @pl.when(t == 0)
            def _():
                @pl.when(j > 0)
                def _():
                    pltpu.make_async_remote_copy(
                        src_ref=pupil_rows(yy), dst_ref=pupil_rows(yy), send_sem=ps_sem.at[0],
                        recv_sem=pr_sem.at[NY - 1 - j], device_id=twin, device_id_type=MESH,
                    ).wait_recv()
                    pupil_core(j).start()

                pupil_core(j).wait_recv()

            rows = pl.ds(pl.multiple_of(yy * 512, 512), 512)
            grad = source_block(
                16, e[rows, :], spec[t], pupil[rows, :], right[...], left[...], left_t[...], right_t[...], cot[t]
            )
            added = dot(et[yy], grad)

            @pl.when(j == 0)
            def _():
                acc[...] = added

            @pl.when(j > 0)
            def _():
                acc[...] += added

            @pl.when(jnp.logical_and(t > 0, j == 0))
            def _():
                turn_x(t - 1)

            @pl.when(jnp.logical_and(t > 0, j == 1))
            def _():
                turn_z(t - 1)

            return inner

        lax.fori_loop(0, NY, one_block, 0)
        send_x[t] = acc[...].astype(BF)
        for d in range(1, NX):
            reduce_x(t, d).start()
        return carry

    lax.fori_loop(0, 4, one_tile, 0)
    turn_x(3)
    turn_z(3)

    for t in range(4):
        for d in range(1, NZ):
            gather_z(t, d).wait_send()
            reduce_z(t, d).wait_send()
        for d in range(1, NX):
            gather_x(t, d).wait_send()
            reduce_x(t, d).wait_send()
    for d in range(1, NY):
        pupil_y(d).wait_send()
    for j in range(NY):
        pupil_core(j).wait_send()


def shards(spectra, cotangent, pupil_field, source_grid, cutoff, stencil, interp_weights, source_weight):
    own_spec = spectra.reshape(4, 8, 2, 2, 128).transpose(0, 1, 3, 2, 4).reshape(4, 16, 256)
    own_pupil = pupil_field.reshape(8, 2, 32, 128).transpose(0, 2, 1, 3).reshape(256, 256)
    vmem = pl.BlockSpec(memory_space=pltpu.VMEM)
    smem = pl.BlockSpec(memory_space=pltpu.SMEM)
    dma = pltpu.SemaphoreType.DMA
    result = pl.pallas_call(
        kernel,
        out_shape=jax.ShapeDtypeStruct((4, 16, 256), F32),
        in_specs=[vmem] * 6 + [smem] * 2 + [vmem] * 4,
        out_specs=vmem,
        scratch_shapes=[
            pltpu.VMEM((4, 512, 256), BF),
            pltpu.VMEM((2048, 256), BF),
            pltpu.VMEM((64, 512), F32),
            pltpu.VMEM((2048, 512), BF),
            pltpu.VMEM((4, 512, 512), BF),
            pltpu.VMEM((512, 256), F32),
            pltpu.VMEM((4, 512, 256), BF),
            pltpu.VMEM((4, 3, 128, 256), BF),
            pltpu.VMEM((4, 128, 256), BF),
            pltpu.VMEM((4, 7, 16, 256), BF),
            dma((4, 7)), dma((4, 7)), dma((4, 3)), dma((4, 3)),
            dma((3,)), dma((3,)), dma((4,)), dma((4,)),
            dma((4, 3)), dma((4, 3)), dma((4, 7)), dma((4, 7)),
        ],
        compiler_params=pltpu.CompilerParams(
            collective_id=0, has_side_effects=True, vmem_limit_bytes=56 << 20
        ),
    )(
        own_spec, own_pupil, cotangent, stencil, interp_weights, source_weight.reshape(64, 1), source_grid, cutoff,
        *[jnp.asarray(v) for v in dft_matrices()],
    )
    return result.reshape(4, 8, 2, 2, 128).transpose(0, 1, 3, 2, 4).reshape(4, 8, 2, 256)


def solution(mesh):
    placed = (
        P("tile", "angle", None, "src"),
        P("tile", None, None),
        P(("angle", "src", "tile"), None, None),
        P(("angle", "src"), None),
        P(("angle", "src")),
        P(("angle", "src"), None),
        P(("angle", "src"), None),
        P(("angle", "src")),
    )
    return jax.shard_map(
        shards, mesh=mesh, in_specs=placed, out_specs=P("tile", "angle", None, "src"), check_vma=False
    )
```

time: 430 us -> 106 us (0.25)
  waiting for transfers between devices: 157 us -> 0 us
  Pallas kernels: 0 us -> 97 us
  local copies, waits for them, and re-layouts: 96.3 us -> 8.42 us
  other arithmetic: 70.1 us -> 0 us
  blocking collectives: 50.7 us -> 0 us
  matrix products: 36.9 us -> 0 us
  between operations: 13.2 us -> 0.01 us
    reduce_scatter x2 -> x0, waiting for transfers between devices: 113 us -> none  [the longest x1 93.5 us: shards(): by_rows = lax.psum_scatter(added, 'src', scatter_dimension=3, tiled=True)]
    pallas_call x0 -> x1, Pallas kernels: none -> 97 us  [shards(): pl.pallas_call(kernel, out_shape=jax.ShapeDtypeStruct((4, 16, 256), F32),...]
    all_gather x1 -> x0, blocking collectives: 50.7 us -> none  [shards(): gathered = lax.all_gather(spectra, 'src', axis=3, tiled=True)]
    all_gather x2 -> x0, waiting for transfers between devices: 43.2 us -> none  [the longest x1 30.9 us: shards(): every_angle = lax.all_gather(gathered, 'angle', axis=1, tiled=True)]
    dot_general x50 -> x0, matrix products: 36.9 us -> none  [the longest x16 13.1 us: gradient_block(): jnp.einsum('btryx,rxqf->btyqf', adjoint, left_table, preferred_element_ty...]
    another operation x22 -> x0, other arithmetic: 31.7 us -> none
    dynamic_update_slice x16 -> x0, other arithmetic: 20.6 us -> none  [shards(): lax.map(one_block, (pieces.reshape(rounds, block_size, 2, orders), mixed....]
    reshape x19 -> x3, local copies, waits for them, and re-layouts: 21.9 us -> 3.59 us  [the longest x1 1.5 us: shards(): result.reshape(4, 8, 2, 2, 128).transpose(0, 1, 3, 2, 4)]
  transfers between devices with their start and end apart: 4 -> 0, of which waited for: 4 -> 0; matrix products, arithmetic and copies ran while one was open for 4% -> 0% of each run, Pallas kernels for 0% -> 0%
where the time goes in v1:
time: 106 us; the launch traced here: 105 us
  Pallas kernels  97 us (92%)
  local copies, waits for them, and re-layouts  8.42 us (8%)
    pallas_call x1, Pallas kernels, shards(): pl.pallas_call(kernel, out_shape=jax.ShapeDtypeStruct((4, 16, 256), F32),...  97 us
    unnamed x8, local copies, waits for them, and re-layouts  4.83 us

profile of v1, /device:TPU:16, one launch (start us, length us, event | category | flops | bytes accessed | tf_op | source)
XLA Modules:
  0.0 105.4 jit_solution(17374679143366244094)
XLA Ops:
  0.0 0.0 copy-start
  0.0 1.4 %copy.16.interp = bf16[64,4]{1,0:T(8,128)(2,1)} copy(bf16[64,4]{0,1:T(4,128)(2,1)} %param.18) | data formatting | bytes 1024 | tf_op args[6]
  1.4 1.4 %reshape.22.own_spec = bf16[4,16,256]{2,1,0:T(8,128)(2,1)} reshape(bf16[4,8,2,2,128]{4,3,2,1,0:T(2,128)(2,1)} %bitcast.17) | data formatting | bytes 65536 | tf_op jit(solution)/shard_map/reshape | solution.py:273
  2.8 1.4 %copy.18.grid = s32[64,2]{1,0:T(8,128)} copy(s32[64,2]{0,1:T(2,128)} %param.15) | data formatting | bytes 1024 | tf_op args[3]
  4.2 0.0 copy-start.1
  4.2 1.4 %copy.15.stencil = s32[64,4]{1,0:T(8,128)} copy(s32[64,4]{0,1:T(4,128)} %param.17) | data formatting | bytes 2048 | tf_op args[5]
  5.6 0.0 copy-done.1
  5.6 0.7 copy.17.weight
  6.3 0.0 copy-done
  6.3 0.7 copy.22
  6.9 97.0 %shard_map.118 = f32[4,16,256]{2,1,0:T(8,128)} custom-call(bf16[4,16,256]{2,1,0:T(8,128)(2,1)} %reshape.22.own_spec, bf16[256,256]{1,0:T(8,128)(2,1)} %bitcast.15, f32[4,128,128]{2,1,0:T(8,128)} %cot.1, s32[64,4]{1,0:T(8,128)} %copy.15.stencil, bf16[64,4]{1,0:T(8,128)(2,1)} %copy.16.interp, f32[64,1]{1,0:T(8,128)} %copy.17.weight, s32[64,2]{1,0:T(8,128)} %copy.18.grid, ...), custom_call_target="tpu_custom_call" | custom-call | tf_op jit(solution)/shard_map/pallas_call | solution.py:278
  103.9 1.5 %reshape.26 = f32[4,8,2,2,128]{4,3,2,1,0:T(2,128)} reshape(f32[4,16,256]{2,1,0:T(8,128)} %shard_map.118) | data formatting | bytes 131072 | tf_op jit(solution)/shard_map/reshape | solution.py:305
Async XLA Ops:
  0.0 6.3 %copy-start = (bf16[8,2,4096]{2,1,0:T(2,128)(2,1)S(1)}, bf16[8,2,4096]{2,1,0:T(2,128)(2,1)}, u32[]{:S(2)}) copy-start(bf16[8,2,4096]{2,1,0:T(2,128)(2,1)} %param.14) | copy-start | bytes 393220
  4.2 1.4 %copy-start.1 = (f32[64]{0:T(128)S(1)}, f32[64]{0:T(128)}, u32[]{:S(2)}) copy-start(f32[64]{0:T(128)} %param.19) | copy-start | bytes 772

commit v2 on v1

v2 whole, which is shorter than its diff:
```python
import functools
import math

import jax
import jax.numpy as jnp
import ml_dtypes
import numpy as np
from jax import lax
from jax.experimental import pallas as pl
from jax.experimental.pallas import tpu as pltpu
from jax.sharding import PartitionSpec as P

FQ = 64
NP = 128
NX, NY, NZ = 4, 4, 8
BF = jnp.bfloat16
F32 = jnp.float32
MESH = pl.DeviceIdType.MESH


def dft_matrices():
    f = np.arange(FQ) - FQ // 2
    phase = np.mod(np.arange(NP)[:, None] * f[None, :], NP) * (2 * math.pi / NP)
    c, s = np.cos(phase) / math.sqrt(FQ), np.sin(phase) / math.sqrt(FQ)
    right = np.zeros((2, 2, 64, 2, 2, 128))
    left = np.zeros((2, 128, 2, 2, 32))
    for p in range(2):
        right[0, p, :, p, 0], right[0, p, :, p, 1] = c.T, s.T
        right[1, p, :, p, 0], right[1, p, :, p, 1] = -s.T, c.T
        left[0, :, p, 0], left[0, :, p, 1] = c[:, p::2], -s[:, p::2]
        left[1, :, p, 0], left[1, :, p, 1] = s[:, p::2], c[:, p::2]
    right, left = right.reshape(256, 512), left.reshape(256, 128)
    return [np.ascontiguousarray(v).astype(ml_dtypes.bfloat16) for v in (right, left, left.T, right.T)]


def dot(a, b):
    return jnp.dot(a, b, preferred_element_type=F32)


def join(values, axis):
    return jnp.concatenate(values, axis=axis)


def source_block(n, h, e, spec, pupil, right, left, left_t, right_t, cot):
    m = n // h
    mixed = [dot(e, spec[x * 128 : x * 128 + 128]) for x in range(NX)]
    pupils, halves = [], []
    for g in range(h):
        p = pupil[g * m * 32 : (g + 1) * m * 32]
        pr, pi = p[:, :128].astype(F32), p[:, 128:].astype(F32)
        pupils.append((pr, pi))
        own = join([mixed[x][s * 8 : s * 8 + 8] for s in range(g * m, (g + 1) * m) for x in range(NX)], 0)
        mr, mi = own[:, :128], own[:, 128:]
        halves.append(join([(pr * mr - pi * mi).astype(BF), (pr * mi + pi * mr).astype(BF)], 1))
    halves = [dot(field, right).astype(BF) for field in halves]
    wide = join([cot, cot], 1)
    wide = join([wide, wide], 0)
    adjoints = []
    for q in range(n // 2):
        pair = []
        for s in (2 * q, 2 * q + 1):
            half, row = halves[s // m], s % m * 32
            pair.append(join([half[row : row + 32, c * 128 : c * 128 + 128] for c in range(4)], 0))
        adjoints.append((dot(left, join(pair, 1)) * wide).astype(BF))
    backs = [dot(left_t, adjoint).astype(BF) for adjoint in adjoints]
    rows = []
    for back in backs:
        for s in range(2):
            rows.append(join([back[c * 32 : c * 32 + 32, s * 128 : s * 128 + 128] for c in range(4)], 1))
    spectra = [dot(join(rows[g * m : (g + 1) * m], 0), right_t) for g in range(h)]
    grads = []
    for (pr, pi), spectrum in zip(pupils, spectra):
        br, bi = spectrum[:, :128], spectrum[:, 128:]
        grads.append(join([pr * br + pi * bi, pr * bi - pi * br], 1))
    return [
        join([grads[s // m][s % m * 32 + x * 8 : s % m * 32 + x * 8 + 8] for s in range(n)], 0).astype(BF)
        for x in range(NX)
    ]


def kernel(
    raw_spec, raw_pupil, cot, stencil, interp, weight, grid, cutoff, right, left, left_t, right_t,
    out,
    own_spec, spec, pupil, e, et, acc, send_x, recv_x, send_z, recv_z,
    zs_sem, zr_sem, xs_sem, xr_sem, ps_sem, pr_sem, cs_sem, cr_sem, rxs_sem, rxr_sem, rzs_sem, rzr_sem,
):
    angle, src, tile = lax.axis_index("angle"), lax.axis_index("src"), lax.axis_index("tile")
    x, z = src // 4, angle * 4 + lax.rem(src, 4)
    y, core = tile // 2, lax.rem(tile, 2)

    def at_x(d):
        return {"src": lax.rem(x + d, NX) * 4 + lax.rem(src, 4)}

    def at_z(d):
        w = lax.rem(z + d, NZ)
        return {"angle": w // 4, "src": x * 4 + lax.rem(w, 4)}

    def at_y(d):
        return {"tile": lax.rem(y + d, NY) * 2 + core}

    twin = {"tile": y * 2 + 1 - core}
    peers = [at_z(d) for d in (4, 3, 5, 2, 6, 1, 7)] + [at_x(d) for d in (2, 1, 3)] + [at_y(d) for d in (2, 1, 3)] + [twin]
    barrier = pltpu.get_barrier_semaphore()
    for peer in peers:
        pl.semaphore_signal(barrier, inc=1, device_id=peer, device_id_type=MESH)

    for t in range(4):
        part = raw_spec[t * 16 : t * 16 + 16]
        own_spec[t] = join([part[:, 0], part[:, 1]], 1)

    lane = lax.broadcasted_iota(jnp.int32, (32, 128), 1)
    fa = 2 * lax.broadcasted_iota(jnp.int32, (32, 128), 0) + (lane >> 6) - 32
    fb = (lane & 63) - 32

    def mask(s8, carry):
        s = tile * 8 + s8
        da, db = fa + grid[0, s], fb + grid[1, s]
        inside = da * da + db * db <= cutoff[s]
        inside = join([inside, inside], 1)
        part = raw_pupil[pl.ds(pl.multiple_of(s8 * 32, 32), 32)]
        value = join([part[:, 0], part[:, 1]], 1).astype(F32)
        pupil[pl.ds(pl.multiple_of(s * 32, 32), 32), :] = jnp.where(inside, value, 0.0).astype(BF)
        return carry

    lax.fori_loop(0, 8, mask, 0)

    c = lax.broadcasted_iota(jnp.int32, (128, 64), 0)
    k_of = (c >> 6) * 8 + ((c >> 1) & 7)
    mix = jnp.zeros((128, 64), F32)
    for j in range(4):
        mix += jnp.where(stencil[j : j + 1, :] == k_of, interp[j : j + 1, :].astype(F32), 0.0)
    scaled = (mix * (weight[...] * (2.0 / math.sqrt(2048)))).astype(BF)
    mix = mix.astype(BF)
    c = lax.broadcasted_iota(jnp.int32, (128, 256), 0)
    col = lax.broadcasted_iota(jnp.int32, (128, 256), 1)
    hit = (col & 7) == ((c >> 4) & 3) * 2 + (c & 1)
    source_at = lax.broadcasted_iota(jnp.int32, (64, 256), 0)
    source_of = lax.broadcasted_iota(jnp.int32, (64, 256), 1) >> 3
    for k in range(2):
        pick = (source_of + k * 32 == source_at).astype(BF)
        et[k] = jnp.where(hit, dot(scaled, pick), 0.0).astype(BF)
        e[k] = jnp.where(hit, dot(mix, pick), 0.0).T.astype(BF)

    pl.semaphore_wait(barrier, len(peers))

    def remote(src_ref, dst_ref, send, recv, peer):
        return pltpu.make_async_remote_copy(
            src_ref=src_ref, dst_ref=dst_ref, send_sem=send, recv_sem=recv, device_id=peer, device_id_type=MESH
        )

    zrows = pl.ds(pl.multiple_of(x * 128 + z * 16, 16), 16)
    xrows = pl.ds(pl.multiple_of(x * 128, 128), 128)

    def gather_z(t, d):
        return remote(own_spec.at[t], spec.at[t, zrows, :], zs_sem.at[t, d - 1], zr_sem.at[t, d - 1], at_z(d))

    def gather_x(t, d):
        rows = spec.at[t, xrows, :]
        return remote(rows, rows, xs_sem.at[t, d - 1], xr_sem.at[t, d - 1], at_x(d))

    def pupil_rows(yy):
        return pupil.at[pl.ds(pl.multiple_of((yy * 2 + core) * 256, 256), 256), :]

    def pupil_y(d):
        return remote(pupil_rows(y), pupil_rows(y), ps_sem.at[d - 1], pr_sem.at[d - 1], at_y(d))

    def pupil_core(j):
        rows = pupil_rows(lax.rem(y + j, NY))
        return remote(rows, rows, cs_sem.at[j], cr_sem.at[j], twin)

    for t in range(4):
        for d in (4, 3, 5, 2, 6, 1, 7):
            gather_z(t, d).start()
        if t == 0:
            for d in range(1, NY):
                pupil_y(d).start()
            pupil_core(0).start()
    for t in range(4):
        spec[t, zrows, :] = own_spec[t]

    for t in range(4):
        for d in range(1, NZ):
            gather_z(t, d).wait_recv()
        for d in (2, 1, 3):
            gather_x(t, d).start()
        if t == 0:
            for d in range(1, NY):
                pupil_y(d).wait_recv()
                pupil_core(NY - d).start()

    def reduce_x(t, d):
        to = lax.rem(x + d, NX)
        rows = send_x.at[t, pl.ds(pl.multiple_of(to * 128, 128), 128), :]
        return remote(rows, recv_x.at[t, d - 1], rxs_sem.at[t, d - 1], rxr_sem.at[t, d - 1], at_x(d))

    def reduce_z(t, d):
        to = lax.rem(z + d, NZ)
        rows = send_z.at[t, pl.ds(pl.multiple_of(to * 16, 16), 16), :]
        return remote(rows, recv_z.at[t, d - 1], rzs_sem.at[t, d - 1], rzr_sem.at[t, d - 1], at_z(d))

    def turn_x(t):
        total = send_x[t, xrows, :].astype(F32)
        for d in range(1, NX):
            reduce_x(t, d).wait_recv()
        for d in range(1, NX):
            total += recv_x[t, d - 1].astype(F32)
        send_z[t] = total.astype(BF)
        for d in (4, 3, 5, 2, 6, 1, 7):
            reduce_z(t, d).start()

    def turn_z(t):
        total = send_z[t, pl.ds(pl.multiple_of(z * 16, 16), 16), :].astype(F32)
        for d in range(1, NZ):
            reduce_z(t, d).wait_recv()
        for d in range(1, NZ):
            total += recv_z[t, d - 1].astype(F32)
        out[t] = total

    def one_block(b, carry):
        t, k = b // 2, lax.rem(b, 2)

        @pl.when(k == 0)
        def _():
            for d in range(1, NX):
                gather_x(t, d).wait_recv()

        @pl.when(b == 0)
        def _():
            for j in range(NY):
                pupil_core(j).wait_recv()

        rows = pl.ds(pl.multiple_of(k * 1024, 1024), 1024)
        grads = source_block(
            32, 4, e[k], spec[t], pupil[rows, :], right[...], left[...], left_t[...], right_t[...], cot[t]
        )
        added = [dot(et[k], g) for g in grads]

        @pl.when(k == 0)
        def _():
            for i in range(NX):
                acc[i * 128 : i * 128 + 128, :] = added[i]

        @pl.when(k == 1)
        def _():
            for i in range(NX):
                send_x[t, i * 128 : i * 128 + 128, :] = (acc[i * 128 : i * 128 + 128, :] + added[i]).astype(BF)
            for d in (2, 1, 3):
                reduce_x(t, d).start()

        @pl.when(b == 4)
        def _():
            turn_x(0)

        @pl.when(b == 6)
        def _():
            turn_x(1)

        return carry

    lax.fori_loop(0, 8, one_block, 0)
    turn_x(2)
    turn_x(3)
    for t in range(4):
        turn_z(t)

    for t in range(4):
        for d in range(1, NZ):
            gather_z(t, d).wait_send()
            reduce_z(t, d).wait_send()
        for d in range(1, NX):
            gather_x(t, d).wait_send()
            reduce_x(t, d).wait_send()
    for d in range(1, NY):
        pupil_y(d).wait_send()
    for j in range(NY):
        pupil_core(j).wait_send()


def shards(spectra, cotangent, pupil_field, source_grid, cutoff, stencil, interp_weights, source_weight):
    own_spec = spectra.reshape(4, 8, 2, 2, 128).transpose(0, 1, 3, 2, 4).reshape(64, 2, 128)
    own_pupil = pupil_field.reshape(8, 2, 32, 128).transpose(0, 2, 1, 3).reshape(256, 2, 128)
    vmem = pl.BlockSpec(memory_space=pltpu.VMEM)
    smem = pl.BlockSpec(memory_space=pltpu.SMEM)
    dma = pltpu.SemaphoreType.DMA
    result = pl.pallas_call(
        kernel,
        out_shape=jax.ShapeDtypeStruct((4, 16, 256), F32),
        in_specs=[vmem] * 6 + [smem] * 2 + [vmem] * 4,
        out_specs=vmem,
        scratch_shapes=[
            pltpu.VMEM((4, 16, 256), BF),
            pltpu.VMEM((4, 512, 256), BF),
            pltpu.VMEM((2048, 256), BF),
            pltpu.VMEM((2, 256, 128), BF),
            pltpu.VMEM((2, 128, 256), BF),
            pltpu.VMEM((512, 256), F32),
            pltpu.VMEM((4, 512, 256), BF),
            pltpu.VMEM((4, 3, 128, 256), BF),
            pltpu.VMEM((4, 128, 256), BF),
            pltpu.VMEM((4, 7, 16, 256), BF),
            dma((4, 7)), dma((4, 7)), dma((4, 3)), dma((4, 3)),
            dma((3,)), dma((3,)), dma((4,)), dma((4,)),
            dma((4, 3)), dma((4, 3)), dma((4, 7)), dma((4, 7)),
        ],
        compiler_params=pltpu.CompilerParams(
            collective_id=0, has_side_effects=True, vmem_limit_bytes=56 << 20
        ),
    )(
        own_spec, own_pupil, cotangent, stencil.T, interp_weights.T, source_weight.reshape(1, 64), source_grid.T, cutoff,
        *[jnp.asarray(v) for v in dft_matrices()],
    )
    return result.reshape(4, 8, 2, 2, 128).transpose(0, 1, 3, 2, 4).reshape(4, 8, 2, 256)


def solution(mesh):
    placed = (
        P("tile", "angle", None, "src"),
        P("tile", None, None),
        P(("angle", "src", "tile"), None, None),
        P(("angle", "src"), None),
        P(("angle", "src")),
        P(("angle", "src"), None),
        P(("angle", "src"), None),
        P(("angle", "src")),
    )
    return jax.shard_map(
        shards, mesh=mesh, in_specs=placed, out_specs=P("tile", "angle", None, "src"), check_vma=False
    )
```

time: 106 us -> 50.7 us (0.48)
  Pallas kernels: 97 us -> 49.1 us
  local copies, waits for them, and re-layouts: 8.42 us -> 1.5 us
    pallas_call x1, Pallas kernels: 97 us -> 49.1 us  [shards(): pl.pallas_call(kernel, out_shape=jax.ShapeDtypeStruct((4, 16, 256), F32),...]
    unnamed x8 -> x0, local copies, waits for them, and re-layouts: 4.83 us -> none
    reshape x2 -> x0, local copies, waits for them, and re-layouts: 2.09 us -> none  [the longest x1 1.4 us: shards(): spectra.reshape(4, 8, 2, 2, 128).transpose(0, 1, 3, 2, 4)]
where the time goes in v2:
time: 50.7 us; the launch traced here: 50.6 us
  Pallas kernels  49.1 us (97%)
  local copies, waits for them, and re-layouts  1.5 us (3%)
    pallas_call x1, Pallas kernels, shards(): pl.pallas_call(kernel, out_shape=jax.ShapeDtypeStruct((4, 16, 256), F32),...  49.1 us
    reshape x1, local copies, waits for them, and re-layouts, shards(): result.reshape(4, 8, 2, 2, 128).transpose(0, 1, 3, 2, 4)  1.5 us

profile of v2, /device:TPU:16, one launch (start us, length us, event | category | flops | bytes accessed | tf_op | source)
XLA Modules:
  0.0 50.6 jit_solution(1439724692121557835)
XLA Ops:
  0.0 49.1 %shard_map.118 = f32[4,16,256]{2,1,0:T(8,128)} custom-call(bf16[64,2,128]{2,1,0:T(2,128)(2,1)} %bitcast.18, bf16[256,2,128]{2,1,0:T(2,128)(2,1)} %bitcast.17, f32[4,128,128]{2,1,0:T(8,128)} %cot.1, s32[4,64]{1,0:T(4,128)} %bitcast.19, bf16[4,64]{1,0:T(4,128)(2,1)} %bitcast.20, f32[1,64]{1,0:T(1,128)} %bitcast.22, s32[2,64]{1,0:T(2,128)} %bitcast.21, ...), custom_call_target="tpu_custom_call" | custom-call | tf_op jit(solution)/shard_map/pallas_call | solution.py:285
  49.1 1.5 %reshape.26 = f32[4,8,2,2,128]{4,3,2,1,0:T(2,128)} reshape(f32[4,16,256]{2,1,0:T(8,128)} %shard_map.118) | data formatting | bytes 131072 | tf_op jit(solution)/shard_map/reshape | solution.py:312

commit v3 on v2

--- a/solution.py
+++ b/solution.py
@@ -16,6 +16,7 @@
 BF = jnp.bfloat16
 F32 = jnp.float32
 MESH = pl.DeviceIdType.MESH
+FAR_FIRST = (4, 3, 5, 2, 6, 1, 7)
 
 
 def dft_matrices():
@@ -79,10 +80,12 @@
 
 
 def kernel(
+    spec_hbm, pupil_hbm, cot_hbm, stencil_hbm, interp_hbm, weight_hbm, grid_hbm, cutoff_hbm,
+    right_hbm, left_hbm, left_t_hbm, right_t_hbm,
+    out,
     raw_spec, raw_pupil, cot, stencil, interp, weight, grid, cutoff, right, left, left_t, right_t,
-    out,
     own_spec, spec, pupil, e, et, acc, send_x, recv_x, send_z, recv_z,
-    zs_sem, zr_sem, xs_sem, xr_sem, ps_sem, pr_sem, cs_sem, cr_sem, rxs_sem, rxr_sem, rzs_sem, rzr_sem,
+    in_sem, hello, zs_sem, zr_sem, xs_sem, xr_sem, ps_sem, pr_sem, cs_sem, cr_sem, rxs_sem, rxr_sem, rzs_sem, rzr_sem,
 ):
     angle, src, tile = lax.axis_index("angle"), lax.axis_index("src"), lax.axis_index("tile")
     x, z = src // 4, angle * 4 + lax.rem(src, 4)
@@ -99,18 +102,37 @@
         return {"tile": lax.rem(y + d, NY) * 2 + core}
 
     twin = {"tile": y * 2 + 1 - core}
-    peers = [at_z(d) for d in (4, 3, 5, 2, 6, 1, 7)] + [at_x(d) for d in (2, 1, 3)] + [at_y(d) for d in (2, 1, 3)] + [twin]
+    peers = [at_z(d) for d in FAR_FIRST] + [at_x(d) for d in (2, 1, 3)] + [at_y(d) for d in (2, 1, 3)]
     barrier = pltpu.get_barrier_semaphore()
     for peer in peers:
         pl.semaphore_signal(barrier, inc=1, device_id=peer, device_id_type=MESH)
 
+    @pl.when(core == 0)
+    def _():
+        pl.semaphore_signal(barrier, inc=1, device_id=twin, device_id_type=MESH)
+
+    pairs = [
+        (spec_hbm, raw_spec), (grid_hbm, grid), (cutoff_hbm, cutoff), (pupil_hbm, raw_pupil), (stencil_hbm, stencil),
+        (interp_hbm, interp), (weight_hbm, weight), (right_hbm, right), (left_hbm, left), (cot_hbm, cot),
+        (left_t_hbm, left_t), (right_t_hbm, right_t),
+    ]
+    loads = [pltpu.make_async_copy(a, b, in_sem.at[i]) for i, (a, b) in enumerate(pairs)]
+    for load in loads:
+        load.start()
+
+    loads[0].wait()
     for t in range(4):
         part = raw_spec[t * 16 : t * 16 + 16]
         own_spec[t] = join([part[:, 0], part[:, 1]], 1)
 
+    for load in loads[1:4]:
+        load.wait()
     lane = lax.broadcasted_iota(jnp.int32, (32, 128), 1)
     fa = 2 * lax.broadcasted_iota(jnp.int32, (32, 128), 0) + (lane >> 6) - 32
     fb = (lane & 63) - 32
+
+    def pupil_rows(yy):
+        return pl.ds(pl.multiple_of((core * 4 + yy) * 256, 256), 256)
 
     def mask(s8, carry):
         s = tile * 8 + s8
@@ -119,11 +141,14 @@
         inside = join([inside, inside], 1)
         part = raw_pupil[pl.ds(pl.multiple_of(s8 * 32, 32), 32)]
         value = join([part[:, 0], part[:, 1]], 1).astype(F32)
-        pupil[pl.ds(pl.multiple_of(s * 32, 32), 32), :] = jnp.where(inside, value, 0.0).astype(BF)
+        rows = pl.ds(pl.multiple_of((core * 4 + y) * 256 + s8 * 32, 32), 32)
+        pupil[rows, :] = jnp.where(inside, value, 0.0).astype(BF)
         return carry
 
     lax.fori_loop(0, 8, mask, 0)
 
+    for load in loads[4:7]:
+        load.wait()
     c = lax.broadcasted_iota(jnp.int32, (128, 64), 0)
     k_of = (c >> 6) * 8 + ((c >> 1) & 7)
     mix = jnp.zeros((128, 64), F32)
@@ -135,13 +160,18 @@
     col = lax.broadcasted_iota(jnp.int32, (128, 256), 1)
     hit = (col & 7) == ((c >> 4) & 3) * 2 + (c & 1)
     source_at = lax.broadcasted_iota(jnp.int32, (64, 256), 0)
-    source_of = lax.broadcasted_iota(jnp.int32, (64, 256), 1) >> 3
+    col = lax.broadcasted_iota(jnp.int32, (64, 256), 1)
+    source_of = (col >> 6) * 16 + ((col >> 3) & 7)
     for k in range(2):
-        pick = (source_of + k * 32 == source_at).astype(BF)
+        pick = (source_of + k * 8 == source_at).astype(BF)
         et[k] = jnp.where(hit, dot(scaled, pick), 0.0).astype(BF)
         e[k] = jnp.where(hit, dot(mix, pick), 0.0).T.astype(BF)
 
-    pl.semaphore_wait(barrier, len(peers))
+    pl.semaphore_wait(barrier, len(peers) + core)
+
+    @pl.when(core == 1)
+    def _():
+        pl.semaphore_signal(hello, inc=1, device_id=twin, device_id_type=MESH)
 
     def remote(src_ref, dst_ref, send, recv, peer):
         return pltpu.make_async_remote_copy(
@@ -158,55 +188,63 @@
         rows = spec.at[t, xrows, :]
         return remote(rows, rows, xs_sem.at[t, d - 1], xr_sem.at[t, d - 1], at_x(d))
 
-    def pupil_rows(yy):
-        return pupil.at[pl.ds(pl.multiple_of((yy * 2 + core) * 256, 256), 256), :]
-
     def pupil_y(d):
-        return remote(pupil_rows(y), pupil_rows(y), ps_sem.at[d - 1], pr_sem.at[d - 1], at_y(d))
+        rows = pupil.at[pupil_rows(y), :]
+        return remote(rows, rows, ps_sem.at[d - 1], pr_sem.at[d - 1], at_y(d))
 
     def pupil_core(j):
-        rows = pupil_rows(lax.rem(y + j, NY))
+        rows = pupil.at[pupil_rows(lax.rem(y + j, NY)), :]
         return remote(rows, rows, cs_sem.at[j], cr_sem.at[j], twin)
 
     for t in range(4):
-        for d in (4, 3, 5, 2, 6, 1, 7):
+        for d in FAR_FIRST:
             gather_z(t, d).start()
         if t == 0:
-            for d in range(1, NY):
+            for d in (2, 1, 3):
                 pupil_y(d).start()
-            pupil_core(0).start()
     for t in range(4):
         spec[t, zrows, :] = own_spec[t]
+    for load in loads[7:]:
+        load.wait()
 
     for t in range(4):
         for d in range(1, NZ):
             gather_z(t, d).wait_recv()
         for d in (2, 1, 3):
             gather_x(t, d).start()
-        if t == 0:
-            for d in range(1, NY):
-                pupil_y(d).wait_recv()
-                pupil_core(NY - d).start()
+
+    @pl.when(core == 0)
+    def _():
+        pl.semaphore_wait(hello, 1)
+
+    pupil_core(0).start()
+    for d in range(1, NY):
+        pupil_y(d).wait_recv()
+        pupil_core(NY - d).start()
 
     def reduce_x(t, d):
         to = lax.rem(x + d, NX)
         rows = send_x.at[t, pl.ds(pl.multiple_of(to * 128, 128), 128), :]
         return remote(rows, recv_x.at[t, d - 1], rxs_sem.at[t, d - 1], rxr_sem.at[t, d - 1], at_x(d))
 
+    def z_block(d):
+        return lax.rem(z + d, NZ) * 16
+
     def reduce_z(t, d):
-        to = lax.rem(z + d, NZ)
-        rows = send_z.at[t, pl.ds(pl.multiple_of(to * 16, 16), 16), :]
+        rows = send_z.at[t, pl.ds(pl.multiple_of(z_block(d), 16), 16), :]
         return remote(rows, recv_z.at[t, d - 1], rzs_sem.at[t, d - 1], rzr_sem.at[t, d - 1], at_z(d))
 
     def turn_x(t):
-        total = send_x[t, xrows, :].astype(F32)
         for d in range(1, NX):
             reduce_x(t, d).wait_recv()
-        for d in range(1, NX):
-            total += recv_x[t, d - 1].astype(F32)
-        send_z[t] = total.astype(BF)
-        for d in (4, 3, 5, 2, 6, 1, 7):
-            reduce_z(t, d).start()
+        for d in FAR_FIRST + (0,):
+            rows = pl.ds(pl.multiple_of(z_block(d), 16), 16)
+            total = send_x[t, pl.ds(pl.multiple_of(x * 128 + z_block(d), 16), 16), :].astype(F32)
+            for w in range(NX - 1):
+                total += recv_x[t, w, rows, :].astype(F32)
+            send_z[t, rows, :] = total.astype(BF)
+            if d:
+                reduce_z(t, d).start()
 
     def turn_z(t):
         total = send_z[t, pl.ds(pl.multiple_of(z * 16, 16), 16), :].astype(F32)
@@ -218,22 +256,23 @@
 
     def one_block(b, carry):
         t, k = b // 2, lax.rem(b, 2)
+        half = lax.rem(core + k, 2)
 
         @pl.when(k == 0)
         def _():
             for d in range(1, NX):
                 gather_x(t, d).wait_recv()
 
-        @pl.when(b == 0)
+        @pl.when(b == 1)
         def _():
             for j in range(NY):
                 pupil_core(j).wait_recv()
 
-        rows = pl.ds(pl.multiple_of(k * 1024, 1024), 1024)
+        rows = pl.ds(pl.multiple_of(half * 1024, 1024), 1024)
         grads = source_block(
-            32, 4, e[k], spec[t], pupil[rows, :], right[...], left[...], left_t[...], right_t[...], cot[t]
+            32, 4, e[half], spec[t], pupil[rows, :], right[...], left[...], left_t[...], right_t[...], cot[t]
         )
-        added = [dot(et[k], g) for g in grads]
+        added = [dot(et[half], g) for g in grads]
 
         @pl.when(k == 0)
         def _():
@@ -259,9 +298,11 @@
 
     lax.fori_loop(0, 8, one_block, 0)
     turn_x(2)
+    turn_z(0)
+    turn_z(1)
     turn_x(3)
-    for t in range(4):
-        turn_z(t)
+    turn_z(2)
+    turn_z(3)
 
     for t in range(4):
         for d in range(1, NZ):
@@ -280,14 +321,26 @@
     own_spec = spectra.reshape(4, 8, 2, 2, 128).transpose(0, 1, 3, 2, 4).reshape(64, 2, 128)
     own_pupil = pupil_field.reshape(8, 2, 32, 128).transpose(0, 2, 1, 3).reshape(256, 2, 128)
     vmem = pl.BlockSpec(memory_space=pltpu.VMEM)
-    smem = pl.BlockSpec(memory_space=pltpu.SMEM)
+    hbm = pl.BlockSpec(memory_space=pl.ANY)
     dma = pltpu.SemaphoreType.DMA
     result = pl.pallas_call(
         kernel,
         out_shape=jax.ShapeDtypeStruct((4, 16, 256), F32),
-        in_specs=[vmem] * 6 + [smem] * 2 + [vmem] * 4,
+        in_specs=[hbm] * 12,
         out_specs=vmem,
         scratch_shapes=[
+            pltpu.VMEM((64, 2, 128), BF),
+            pltpu.VMEM((256, 2, 128), BF),
+            pltpu.VMEM((4, 128, 128), F32),
+            pltpu.VMEM((4, 64), jnp.int32),
+            pltpu.VMEM((4, 64), BF),
+            pltpu.VMEM((1, 64), F32),
+            pltpu.SMEM((2, 64), jnp.int32),
+            pltpu.SMEM((64,), jnp.int32),
+            pltpu.VMEM((256, 512), BF),
+            pltpu.VMEM((256, 128), BF),
+            pltpu.VMEM((128, 256), BF),
+            pltpu.VMEM((512, 256), BF),
             pltpu.VMEM((4, 16, 256), BF),
             pltpu.VMEM((4, 512, 256), BF),
             pltpu.VMEM((2048, 256), BF),
@@ -298,6 +351,7 @@
             pltpu.VMEM((4, 3, 128, 256), BF),
             pltpu.VMEM((4, 128, 256), BF),
             pltpu.VMEM((4, 7, 16, 256), BF),
+            dma((12,)), pltpu.SemaphoreType.REGULAR,
             dma((4, 7)), dma((4, 7)), dma((4, 3)), dma((4, 3)),
             dma((3,)), dma((3,)), dma((4,)), dma((4,)),
             dma((4, 3)), dma((4, 3)), dma((4, 7)), dma((4, 7)),

time: 50.7 us -> 48.8 us (0.963)
  Pallas kernels: 49.1 us -> 47.2 us
    pallas_call x1, Pallas kernels: 49.1 us -> 47.2 us  [shards(): pl.pallas_call(kernel, out_shape=jax.ShapeDtypeStruct((4, 16, 256), F32),...]
where the time goes in v3:
time: 48.8 us; the launch traced here: 48.7 us
  Pallas kernels  47.2 us (97%)
  local copies, waits for them, and re-layouts  1.5 us (3%)
    pallas_call x1, Pallas kernels, shards(): pl.pallas_call(kernel, out_shape=jax.ShapeDtypeStruct((4, 16, 256), F32),...  47.2 us
    reshape x1, local copies, waits for them, and re-layouts, shards(): result.reshape(4, 8, 2, 2, 128).transpose(0, 1, 3, 2, 4)  1.5 us

profile of v3, /device:TPU:16, one launch (start us, length us, event | category | flops | bytes accessed | tf_op | source)
XLA Modules:
  0.0 48.7 jit_solution(14069556736207418051)
XLA Ops:
  0.0 47.2 %shard_map.118 = f32[4,16,256]{2,1,0:T(8,128)} custom-call(bf16[64,2,128]{2,1,0:T(2,128)(2,1)} %bitcast.18, bf16[256,2,128]{2,1,0:T(2,128)(2,1)} %bitcast.17, f32[4,128,128]{2,1,0:T(8,128)} %cot_hbm.1, s32[4,64]{1,0:T(4,128)} %bitcast.19, bf16[4,64]{1,0:T(4,128)(2,1)} %bitcast.20, f32[1,64]{1,0:T(1,128)} %bitcast.22, s32[2,64]{1,0:T(2,128)} %bitcast.21, ...), custom_call_target="tpu_custom_call" | custom-call | tf_op jit(solution)/shard_map/pallas_call | solution.py:326
  47.2 1.5 %reshape.26 = f32[4,8,2,2,128]{4,3,2,1,0:T(2,128)} reshape(f32[4,16,256]{2,1,0:T(8,128)} %shard_map.118) | data formatting | bytes 131072 | tf_op jit(solution)/shard_map/reshape | solution.py:366

commit v4 on v3

--- a/solution.py
+++ b/solution.py
@@ -17,6 +17,7 @@
 F32 = jnp.float32
 MESH = pl.DeviceIdType.MESH
 FAR_FIRST = (4, 3, 5, 2, 6, 1, 7)
+GROUPS = {32: 4, 64: 8}
 
 
 def dft_matrices():
@@ -125,14 +126,63 @@
         part = raw_spec[t * 16 : t * 16 + 16]
         own_spec[t] = join([part[:, 0], part[:, 1]], 1)
 
+    pl.semaphore_wait(barrier, len(peers) + core)
+
+    @pl.when(core == 1)
+    def _():
+        pl.semaphore_signal(hello, inc=1, device_id=twin, device_id_type=MESH)
+
+    def remote(src_ref, dst_ref, send, recv, peer):
+        return pltpu.make_async_remote_copy(
+            src_ref=src_ref, dst_ref=dst_ref, send_sem=send, recv_sem=recv, device_id=peer, device_id_type=MESH
+        )
+
+    zrows = pl.ds(pl.multiple_of(z * 16, 16), 16)
+    xrows = pl.ds(pl.multiple_of(x * 128, 128), 128)
+
+    def gather_z(t, d):
+        return remote(own_spec.at[t], spec.at[t, x, zrows, :], zs_sem.at[t, d - 1], zr_sem.at[t, d - 1], at_z(d))
+
+    def gather_x(t, d):
+        rows = spec.at[t, x]
+        return remote(rows, rows, xs_sem.at[t, d - 1], xr_sem.at[t, d - 1], at_x(d))
+
+    def first_x(t, d):
+        return remote(own_spec.at[t], spec.at[t, x, zrows, :], xs_sem.at[t, d - 1], xr_sem.at[t, d - 1], at_x(d))
+
+    def then_z(t, d):
+        rows = spec.at[t, :, zrows, :]
+        return remote(rows, rows, zs_sem.at[t, d - 1], zr_sem.at[t, d - 1], at_z(d))
+
+    def forward(t):
+        for d in range(1, NX):
+            first_x(t, d).wait_recv()
+        for d in FAR_FIRST:
+            then_z(t, d).start()
+
+    def pupil_rows(yy):
+        return pl.ds(pl.multiple_of((core * 4 + yy) * 256, 256), 256)
+
+    def pupil_y(d):
+        rows = pupil.at[pupil_rows(y), :]
+        return remote(rows, rows, ps_sem.at[d - 1], pr_sem.at[d - 1], at_y(d))
+
+    def pupil_core(j):
+        rows = pupil.at[pupil_rows(lax.rem(y + j, NY)), :]
+        return remote(rows, rows, cs_sem.at[j], cr_sem.at[j], twin)
+
+    for d in FAR_FIRST:
+        gather_z(0, d).start()
+    for d in (2, 1, 3):
+        first_x(2, d).start()
+    for d in (2, 1, 3):
+        first_x(3, d).start()
+
     for load in loads[1:4]:
         load.wait()
     lane = lax.broadcasted_iota(jnp.int32, (32, 128), 1)
     fa = 2 * lax.broadcasted_iota(jnp.int32, (32, 128), 0) + (lane >> 6) - 32
     fb = (lane & 63) - 32
-
-    def pupil_rows(yy):
-        return pl.ds(pl.multiple_of((core * 4 + yy) * 256, 256), 256)
 
     def mask(s8, carry):
         s = tile * 8 + s8
@@ -146,6 +196,13 @@
         return carry
 
     lax.fori_loop(0, 8, mask, 0)
+
+    for d in (2, 1, 3):
+        pupil_y(d).start()
+    for d in FAR_FIRST:
+        gather_z(1, d).start()
+    for t in range(4):
+        spec[t, x, zrows, :] = own_spec[t]
 
     for load in loads[4:7]:
         load.wait()
@@ -164,54 +221,23 @@
     source_of = (col >> 6) * 16 + ((col >> 3) & 7)
     for k in range(2):
         pick = (source_of + k * 8 == source_at).astype(BF)
-        et[k] = jnp.where(hit, dot(scaled, pick), 0.0).astype(BF)
-        e[k] = jnp.where(hit, dot(mix, pick), 0.0).T.astype(BF)
-
-    pl.semaphore_wait(barrier, len(peers) + core)
-
-    @pl.when(core == 1)
-    def _():
-        pl.semaphore_signal(hello, inc=1, device_id=twin, device_id_type=MESH)
-
-    def remote(src_ref, dst_ref, send, recv, peer):
-        return pltpu.make_async_remote_copy(
-            src_ref=src_ref, dst_ref=dst_ref, send_sem=send, recv_sem=recv, device_id=peer, device_id_type=MESH
-        )
-
-    zrows = pl.ds(pl.multiple_of(x * 128 + z * 16, 16), 16)
-    xrows = pl.ds(pl.multiple_of(x * 128, 128), 128)
-
-    def gather_z(t, d):
-        return remote(own_spec.at[t], spec.at[t, zrows, :], zs_sem.at[t, d - 1], zr_sem.at[t, d - 1], at_z(d))
-
-    def gather_x(t, d):
-        rows = spec.at[t, xrows, :]
-        return remote(rows, rows, xs_sem.at[t, d - 1], xr_sem.at[t, d - 1], at_x(d))
-
-    def pupil_y(d):
-        rows = pupil.at[pupil_rows(y), :]
-        return remote(rows, rows, ps_sem.at[d - 1], pr_sem.at[d - 1], at_y(d))
-
-    def pupil_core(j):
-        rows = pupil.at[pupil_rows(lax.rem(y + j, NY)), :]
-        return remote(rows, rows, cs_sem.at[j], cr_sem.at[j], twin)
-
-    for t in range(4):
-        for d in FAR_FIRST:
-            gather_z(t, d).start()
-        if t == 0:
-            for d in (2, 1, 3):
-                pupil_y(d).start()
-    for t in range(4):
-        spec[t, zrows, :] = own_spec[t]
+        et[:, k * 256 : k * 256 + 256] = jnp.where(hit, dot(scaled, pick), 0.0).astype(BF)
+        e[k * 256 : k * 256 + 256, :] = jnp.where(hit, dot(mix, pick), 0.0).T.astype(BF)
+
     for load in loads[7:]:
         load.wait()
 
-    for t in range(4):
-        for d in range(1, NZ):
-            gather_z(t, d).wait_recv()
-        for d in (2, 1, 3):
-            gather_x(t, d).start()
+    for d in range(1, NZ):
+        gather_z(0, d).wait_recv()
+    for d in (2, 1, 3):
+        gather_x(0, d).start()
+
+    for d in range(1, NZ):
+        gather_z(1, d).wait_recv()
+    for d in (2, 1, 3):
+        gather_x(1, d).start()
+
+    forward(2)
 
     @pl.when(core == 0)
     def _():
@@ -254,49 +280,62 @@
             total += recv_z[t, d - 1].astype(F32)
         out[t] = total
 
-    def one_block(b, carry):
-        t, k = b // 2, lax.rem(b, 2)
-        half = lax.rem(core + k, 2)
-
-        @pl.when(k == 0)
+    def sums(n, first, t):
+        grads = source_block(
+            n, GROUPS[n], e[pl.ds(pl.multiple_of(first * 8, 256), n * 8), :], spec[t].reshape(512, 256),
+            pupil[pl.ds(pl.multiple_of(first * 32, 1024), n * 32), :],
+            right[...], left[...], left_t[...], right_t[...], cot[t],
+        )
+        weights = et[:, pl.ds(pl.multiple_of(first * 8, 256), n * 8)]
+        return [dot(weights, g) for g in grads]
+
+    for d in range(1, NX):
+        gather_x(0, d).wait_recv()
+
+    def first_tile(k, carry):
+        @pl.when(k == 1)
+        def _():
+            forward(3)
+            for j in range(NY):
+                pupil_core(j).wait_recv()
+
+        added = sums(32, lax.rem(core + k, 2) * 32, 0)
+        for i in range(NX):
+            rows = pl.ds(i * 128, 128)
+            acc[rows, :] = acc[rows, :] * k.astype(F32) + added[i]
+        return carry
+
+    acc[...] = jnp.zeros_like(acc)
+    lax.fori_loop(0, 2, first_tile, 0)
+    send_x[0] = acc[...].astype(BF)
+    for d in (2, 1, 3):
+        reduce_x(0, d).start()
+
+    def one_tile(t, carry):
+        @pl.when(t == 1)
         def _():
             for d in range(1, NX):
                 gather_x(t, d).wait_recv()
 
-        @pl.when(b == 1)
+        @pl.when(t > 1)
         def _():
-            for j in range(NY):
-                pupil_core(j).wait_recv()
-
-        rows = pl.ds(pl.multiple_of(half * 1024, 1024), 1024)
-        grads = source_block(
-            32, 4, e[half], spec[t], pupil[rows, :], right[...], left[...], left_t[...], right_t[...], cot[t]
-        )
-        added = [dot(et[half], g) for g in grads]
-
-        @pl.when(k == 0)
-        def _():
-            for i in range(NX):
-                acc[i * 128 : i * 128 + 128, :] = added[i]
-
-        @pl.when(k == 1)
-        def _():
-            for i in range(NX):
-                send_x[t, i * 128 : i * 128 + 128, :] = (acc[i * 128 : i * 128 + 128, :] + added[i]).astype(BF)
-            for d in (2, 1, 3):
-                reduce_x(t, d).start()
-
-        @pl.when(b == 4)
+            for d in range(1, NZ):
+                then_z(t, d).wait_recv()
+
+        added = sums(64, 0, t)
+        for i in range(NX):
+            send_x[t, i * 128 : i * 128 + 128, :] = added[i].astype(BF)
+        for d in (2, 1, 3):
+            reduce_x(t, d).start()
+
+        @pl.when(t == 2)
         def _():
             turn_x(0)
 
-        @pl.when(b == 6)
-        def _():
-            turn_x(1)
-
         return carry
 
-    lax.fori_loop(0, 8, one_block, 0)
+    lax.fori_loop(1, 4, one_tile, 0)
+    turn_x(1)
     turn_x(2)
     turn_z(0)
     turn_z(1)
@@ -306,10 +345,10 @@
 
     for t in range(4):
         for d in range(1, NZ):
-            gather_z(t, d).wait_send()
+            (then_z if t in (2, 3) else gather_z)(t, d).wait_send()
             reduce_z(t, d).wait_send()
         for d in range(1, NX):
-            gather_x(t, d).wait_send()
+            (first_x if t in (2, 3) else gather_x)(t, d).wait_send()
             reduce_x(t, d).wait_send()
     for d in range(1, NY):
         pupil_y(d).wait_send()
@@ -342,10 +381,10 @@
             pltpu.VMEM((128, 256), BF),
             pltpu.VMEM((512, 256), BF),
             pltpu.VMEM((4, 16, 256), BF),
-            pltpu.VMEM((4, 512, 256), BF),
+            pltpu.VMEM((4, NX, 128, 256), BF),
             pltpu.VMEM((2048, 256), BF),
-            pltpu.VMEM((2, 256, 128), BF),
-            pltpu.VMEM((2, 128, 256), BF),
+            pltpu.VMEM((512, 128), BF),
+            pltpu.VMEM((128, 512), BF),
             pltpu.VMEM((512, 256), F32),
             pltpu.VMEM((4, 512, 256), BF),
             pltpu.VMEM((4, 3, 128, 256), BF),

time: 48.8 us -> 46.7 us (0.957)
  Pallas kernels: 47.2 us -> 45.1 us
    pallas_call x1, Pallas kernels: 47.2 us -> 45.1 us  [shards(): pl.pallas_call(kernel, out_shape=jax.ShapeDtypeStruct((4, 16, 256), F32),...]
where the time goes in v4:
time: 46.7 us; the launch traced here: 46.6 us
  Pallas kernels  45.1 us (97%)
  local copies, waits for them, and re-layouts  1.5 us (3%)
    pallas_call x1, Pallas kernels, shards(): pl.pallas_call(kernel, out_shape=jax.ShapeDtypeStruct((4, 16, 256), F32),...  45.1 us
    reshape x1, local copies, waits for them, and re-layouts, shards(): result.reshape(4, 8, 2, 2, 128).transpose(0, 1, 3, 2, 4)  1.5 us

profile of v4, /device:TPU:16, one launch (start us, length us, event | category | flops | bytes accessed | tf_op | source)
XLA Modules:
  0.0 46.6 jit_solution(4513998455830333207)
XLA Ops:
  0.0 45.1 %shard_map.118 = f32[4,16,256]{2,1,0:T(8,128)} custom-call(bf16[64,2,128]{2,1,0:T(2,128)(2,1)} %bitcast.18, bf16[256,2,128]{2,1,0:T(2,128)(2,1)} %bitcast.17, f32[4,128,128]{2,1,0:T(8,128)} %cot_hbm.1, s32[4,64]{1,0:T(4,128)} %bitcast.19, bf16[4,64]{1,0:T(4,128)(2,1)} %bitcast.20, f32[1,64]{1,0:T(1,128)} %bitcast.22, s32[2,64]{1,0:T(2,128)} %bitcast.21, ...), custom_call_target="tpu_custom_call" | custom-call | tf_op jit(solution)/shard_map/pallas_call | solution.py:365
  45.1 1.5 %reshape.26 = f32[4,8,2,2,128]{4,3,2,1,0:T(2,128)} reshape(f32[4,16,256]{2,1,0:T(8,128)} %shard_map.118) | data formatting | bytes 131072 | tf_op jit(solution)/shard_map/reshape | solution.py:405

commit v5 on v4

--- a/solution.py
+++ b/solution.py
@@ -126,58 +126,6 @@
         part = raw_spec[t * 16 : t * 16 + 16]
         own_spec[t] = join([part[:, 0], part[:, 1]], 1)
 
-    pl.semaphore_wait(barrier, len(peers) + core)
-
-    @pl.when(core == 1)
-    def _():
-        pl.semaphore_signal(hello, inc=1, device_id=twin, device_id_type=MESH)
-
-    def remote(src_ref, dst_ref, send, recv, peer):
-        return pltpu.make_async_remote_copy(
-            src_ref=src_ref, dst_ref=dst_ref, send_sem=send, recv_sem=recv, device_id=peer, device_id_type=MESH
-        )
-
-    zrows = pl.ds(pl.multiple_of(z * 16, 16), 16)
-    xrows = pl.ds(pl.multiple_of(x * 128, 128), 128)
-
-    def gather_z(t, d):
-        return remote(own_spec.at[t], spec.at[t, x, zrows, :], zs_sem.at[t, d - 1], zr_sem.at[t, d - 1], at_z(d))
-
-    def gather_x(t, d):
-        rows = spec.at[t, x]
-        return remote(rows, rows, xs_sem.at[t, d - 1], xr_sem.at[t, d - 1], at_x(d))
-
-    def first_x(t, d):
-        return remote(own_spec.at[t], spec.at[t, x, zrows, :], xs_sem.at[t, d - 1], xr_sem.at[t, d - 1], at_x(d))
-
-    def then_z(t, d):
-        rows = spec.at[t, :, zrows, :]
-        return remote(rows, rows, zs_sem.at[t, d - 1], zr_sem.at[t, d - 1], at_z(d))
-
-    def forward(t):
-        for d in range(1, NX):
-            first_x(t, d).wait_recv()
-        for d in FAR_FIRST:
-            then_z(t, d).start()
-
-    def pupil_rows(yy):
-        return pl.ds(pl.multiple_of((core * 4 + yy) * 256, 256), 256)
-
-    def pupil_y(d):
-        rows = pupil.at[pupil_rows(y), :]
-        return remote(rows, rows, ps_sem.at[d - 1], pr_sem.at[d - 1], at_y(d))
-
-    def pupil_core(j):
-        rows = pupil.at[pupil_rows(lax.rem(y + j, NY)), :]
-        return remote(rows, rows, cs_sem.at[j], cr_sem.at[j], twin)
-
-    for d in FAR_FIRST:
-        gather_z(0, d).start()
-    for d in (2, 1, 3):
-        first_x(2, d).start()
-    for d in (2, 1, 3):
-        first_x(3, d).start()
-
     for load in loads[1:4]:
         load.wait()
     lane = lax.broadcasted_iota(jnp.int32, (32, 128), 1)
@@ -196,6 +144,58 @@
         return carry
 
     lax.fori_loop(0, 8, mask, 0)
+
+    pl.semaphore_wait(barrier, len(peers) + core)
+
+    @pl.when(core == 1)
+    def _():
+        pl.semaphore_signal(hello, inc=1, device_id=twin, device_id_type=MESH)
+
+    def remote(src_ref, dst_ref, send, recv, peer):
+        return pltpu.make_async_remote_copy(
+            src_ref=src_ref, dst_ref=dst_ref, send_sem=send, recv_sem=recv, device_id=peer, device_id_type=MESH
+        )
+
+    zrows = pl.ds(pl.multiple_of(z * 16, 16), 16)
+    xrows = pl.ds(pl.multiple_of(x * 128, 128), 128)
+
+    def gather_z(t, d):
+        return remote(own_spec.at[t], spec.at[t, x, zrows, :], zs_sem.at[t, d - 1], zr_sem.at[t, d - 1], at_z(d))
+
+    def gather_x(t, d):
+        rows = spec.at[t, x]
+        return remote(rows, rows, xs_sem.at[t, d - 1], xr_sem.at[t, d - 1], at_x(d))
+
+    def first_x(t, d):
+        return remote(own_spec.at[t], spec.at[t, x, zrows, :], xs_sem.at[t, d - 1], xr_sem.at[t, d - 1], at_x(d))
+
+    def then_z(t, d):
+        rows = spec.at[t, :, zrows, :]
+        return remote(rows, rows, zs_sem.at[t, d - 1], zr_sem.at[t, d - 1], at_z(d))
+
+    def forward(t):
+        for d in range(1, NX):
+            first_x(t, d).wait_recv()
+        for d in FAR_FIRST:
+            then_z(t, d).start()
+
+    def pupil_rows(yy):
+        return pl.ds(pl.multiple_of((core * 4 + yy) * 256, 256), 256)
+
+    def pupil_y(d):
+        rows = pupil.at[pupil_rows(y), :]
+        return remote(rows, rows, ps_sem.at[d - 1], pr_sem.at[d - 1], at_y(d))
+
+    def pupil_core(j):
+        rows = pupil.at[pupil_rows(lax.rem(y + j, NY)), :]
+        return remote(rows, rows, cs_sem.at[j], cr_sem.at[j], twin)
+
+    for d in FAR_FIRST:
+        gather_z(0, d).start()
+    for d in (2, 1, 3):
+        first_x(2, d).start()
+    for d in (2, 1, 3):
+        first_x(3, d).start()
 
     for d in (2, 1, 3):
         pupil_y(d).start()
@@ -341,12 +341,11 @@
     turn_z(1)
     turn_x(3)
     turn_z(2)
-    turn_z(3)
-
     for t in range(4):
         for d in range(1, NZ):
             (then_z if t in (2, 3) else gather_z)(t, d).wait_send()
-            reduce_z(t, d).wait_send()
+            if t < 3:
+                reduce_z(t, d).wait_send()
         for d in range(1, NX):
             (first_x if t in (2, 3) else gather_x)(t, d).wait_send()
             reduce_x(t, d).wait_send()
@@ -354,6 +353,9 @@
         pupil_y(d).wait_send()
     for j in range(NY):
         pupil_core(j).wait_send()
+    turn_z(3)
+    for d in range(1, NZ):
+        reduce_z(3, d).wait_send()
 
 
 def shards(spectra, cotangent, pupil_field, source_grid, cutoff, stencil, interp_weights, source_weight):
@@ -364,7 +366,7 @@
     dma = pltpu.SemaphoreType.DMA
     result = pl.pallas_call(
         kernel,
-        out_shape=jax.ShapeDtypeStruct((4, 16, 256), F32),
+        out_shape=pltpu.VMEM((4, 16, 256), F32),
         in_specs=[hbm] * 12,
         out_specs=vmem,
         scratch_shapes=[

time: 46.7 us -> 45.1 us (0.966)
  local copies, waits for them, and re-layouts: 1.5 us -> 0.66 us
  Pallas kernels: 45.1 us -> 44.3 us
    reshape x1, local copies, waits for them, and re-layouts: 1.5 us -> 0.66 us  [shards(): result.reshape(4, 8, 2, 2, 128).transpose(0, 1, 3, 2, 4)]
    pallas_call x1, Pallas kernels: 45.1 us -> 44.3 us  [shards(): pl.pallas_call(kernel, out_shape=pltpu.VMEM((4, 16, 256), F32), in_specs=...]
where the time goes in v5:
time: 45.1 us; the launch traced here: 45 us
  Pallas kernels  44.3 us (98%)
  local copies, waits for them, and re-layouts  0.66 us (1%)
    pallas_call x1, Pallas kernels, shards(): pl.pallas_call(kernel, out_shape=pltpu.VMEM((4, 16, 256), F32), in_specs=...  44.3 us

profile of v5, /device:TPU:16, one launch (start us, length us, event | category | flops | bytes accessed | tf_op | source)
XLA Modules:
  0.0 45.0 jit_solution(3190133885341950003)
XLA Ops:
  0.0 44.3 %shard_map.118 = f32[4,16,256]{2,1,0:T(8,128)S(1)} custom-call(bf16[64,2,128]{2,1,0:T(2,128)(2,1)} %bitcast.18, bf16[256,2,128]{2,1,0:T(2,128)(2,1)} %bitcast.17, f32[4,128,128]{2,1,0:T(8,128)} %cot_hbm.1, s32[4,64]{1,0:T(4,128)} %bitcast.19, bf16[4,64]{1,0:T(4,128)(2,1)} %bitcast.20, f32[1,64]{1,0:T(1,128)} %bitcast.22, s32[2,64]{1,0:T(2,128)} %bitcast.21, ...), custom_call_target="tpu_custom_call" | custom-call | tf_op jit(solution)/shard_map/pallas_call | solution.py:367
  44.3 0.7 %reshape.26 = f32[4,8,2,2,128]{4,3,2,1,0:T(2,128)} reshape(f32[4,16,256]{2,1,0:T(8,128)S(1)} %shard_map.118) | data formatting | bytes 131072 | tf_op jit(solution)/shard_map/reshape | solution.py:407

commit v6 on v5

--- a/solution.py
+++ b/solution.py
@@ -338,8 +338,8 @@
     turn_x(1)
     turn_x(2)
     turn_z(0)
+    turn_x(3)
     turn_z(1)
-    turn_x(3)
     turn_z(2)
     for t in range(4):
         for d in range(1, NZ):

time: 45.1 us -> 44.5 us (0.987)
  Pallas kernels: 44.3 us -> 43.7 us
    pallas_call x1, Pallas kernels: 44.3 us -> 43.7 us  [shards(): pl.pallas_call(kernel, out_shape=pltpu.VMEM((4, 16, 256), F32), in_specs=...]
where the time goes in v6:
time: 44.5 us; the launch traced here: 44.4 us
  Pallas kernels  43.7 us (98%)
  local copies, waits for them, and re-layouts  0.66 us (1%)
    pallas_call x1, Pallas kernels, shards(): pl.pallas_call(kernel, out_shape=pltpu.VMEM((4, 16, 256), F32), in_specs=...  43.7 us

profile of v6, /device:TPU:16, one launch (start us, length us, event | category | flops | bytes accessed | tf_op | source)
XLA Modules:
  0.0 44.4 jit_solution(16731968211629245896)
XLA Ops:
  0.0 43.7 %shard_map.118 = f32[4,16,256]{2,1,0:T(8,128)S(1)} custom-call(bf16[64,2,128]{2,1,0:T(2,128)(2,1)} %bitcast.18, bf16[256,2,128]{2,1,0:T(2,128)(2,1)} %bitcast.17, f32[4,128,128]{2,1,0:T(8,128)} %cot_hbm.1, s32[4,64]{1,0:T(4,128)} %bitcast.19, bf16[4,64]{1,0:T(4,128)(2,1)} %bitcast.20, f32[1,64]{1,0:T(1,128)} %bitcast.22, s32[2,64]{1,0:T(2,128)} %bitcast.21, ...), custom_call_target="tpu_custom_call" | custom-call | tf_op jit(solution)/shard_map/pallas_call | solution.py:367
  43.7 0.7 %reshape.26 = f32[4,8,2,2,128]{4,3,2,1,0:T(2,128)} reshape(f32[4,16,256]{2,1,0:T(8,128)S(1)} %shard_map.118) | data formatting | bytes 131072 | tf_op jit(solution)/shard_map/reshape | solution.py:407

commit v7 on v6

--- a/solution.py
+++ b/solution.py
@@ -85,8 +85,8 @@
     right_hbm, left_hbm, left_t_hbm, right_t_hbm,
     out,
     raw_spec, raw_pupil, cot, stencil, interp, weight, grid, cutoff, right, left, left_t, right_t,
-    own_spec, spec, pupil, e, et, acc, send_x, recv_x, send_z, recv_z,
-    in_sem, hello, zs_sem, zr_sem, xs_sem, xr_sem, ps_sem, pr_sem, cs_sem, cr_sem, rxs_sem, rxr_sem, rzs_sem, rzr_sem,
+    own_spec, spec, pupil, e, et, acc, send_x, recv_x, send_z, recv_z, recv_far,
+    in_sem, hello, zs_sem, zr_sem, xs_sem, xr_sem, ps_sem, pr_sem, cs_sem, cr_sem, rxs_sem, rxr_sem, rzs_sem, rzr_sem, far_s_sem, far_r_sem,
 ):
     angle, src, tile = lax.axis_index("angle"), lax.axis_index("src"), lax.axis_index("tile")
     x, z = src // 4, angle * 4 + lax.rem(src, 4)
@@ -260,14 +260,21 @@
         rows = send_z.at[t, pl.ds(pl.multiple_of(z_block(d), 16), 16), :]
         return remote(rows, recv_z.at[t, d - 1], rzs_sem.at[t, d - 1], rzr_sem.at[t, d - 1], at_z(d))
 
+    def reduce_far(d):
+        rows = send_x.at[3, pl.ds(pl.multiple_of(lax.rem(x + 2, NX) * 128 + z_block(d), 16), 16), :]
+        w = lax.rem(z + d, NZ)
+        peer = {"angle": w // 4, "src": lax.rem(x + 2, NX) * 4 + lax.rem(w, 4)}
+        return remote(rows, recv_far.at[d], far_s_sem.at[d], far_r_sem.at[d], peer)
+
     def turn_x(t):
-        for d in range(1, NX):
+        steps = (1, 3) if isinstance(t, int) and t == 3 else (1, 2, 3)
+        for d in steps:
             reduce_x(t, d).wait_recv()
         for d in FAR_FIRST + (0,):
             rows = pl.ds(pl.multiple_of(z_block(d), 16), 16)
             total = send_x[t, pl.ds(pl.multiple_of(x * 128 + z_block(d), 16), 16), :].astype(F32)
-            for w in range(NX - 1):
-                total += recv_x[t, w, rows, :].astype(F32)
+            for w in steps:
+                total += recv_x[t, w - 1, rows, :].astype(F32)
             send_z[t, rows, :] = total.astype(BF)
             if d:
                 reduce_z(t, d).start()
@@ -278,6 +285,11 @@
             reduce_z(t, d).wait_recv()
         for d in range(1, NZ):
             total += recv_z[t, d - 1].astype(F32)
+        if t == 3:
+            for d in range(NZ):
+                reduce_far(d).wait_recv()
+            for d in range(NZ):
+                total += recv_far[d].astype(F32)
         out[t] = total
 
     def sums(n, first, t):
@@ -325,8 +337,17 @@
         added = sums(64, 0, t)
         for i in range(NX):
             send_x[t, i * 128 : i * 128 + 128, :] = added[i].astype(BF)
-        for d in (2, 1, 3):
+        for d in (1, 3):
             reduce_x(t, d).start()
+
+        @pl.when(t < 3)
+        def _():
+            reduce_x(t, 2).start()
+
+        @pl.when(t == 3)
+        def _():
+            for d in FAR_FIRST + (0,):
+                reduce_far(d).start()
 
         @pl.when(t == 2)
         def _():
@@ -348,11 +369,14 @@
                 reduce_z(t, d).wait_send()
         for d in range(1, NX):
             (first_x if t in (2, 3) else gather_x)(t, d).wait_send()
-            reduce_x(t, d).wait_send()
+            if t < 3 or d != 2:
+                reduce_x(t, d).wait_send()
     for d in range(1, NY):
         pupil_y(d).wait_send()
     for j in range(NY):
         pupil_core(j).wait_send()
+    for d in range(NZ):
+        reduce_far(d).wait_send()
     turn_z(3)
     for d in range(1, NZ):
         reduce_z(3, d).wait_send()
@@ -392,10 +416,11 @@
             pltpu.VMEM((4, 3, 128, 256), BF),
             pltpu.VMEM((4, 128, 256), BF),
             pltpu.VMEM((4, 7, 16, 256), BF),
+            pltpu.VMEM((8, 16, 256), BF),
             dma((12,)), pltpu.SemaphoreType.REGULAR,
             dma((4, 7)), dma((4, 7)), dma((4, 3)), dma((4, 3)),
             dma((3,)), dma((3,)), dma((4,)), dma((4,)),
-            dma((4, 3)), dma((4, 3)), dma((4, 7)), dma((4, 7)),
+            dma((4, 3)), dma((4, 3)), dma((4, 7)), dma((4, 7)), dma((8,)), dma((8,)),
         ],
         compiler_params=pltpu.CompilerParams(
             collective_id=0, has_side_effects=True, vmem_limit_bytes=56 << 20

time: 44.5 us -> 44.2 us (level)
  Pallas kernels: 43.7 us -> 43.2 us
    pallas_call x1, Pallas kernels: 43.7 us -> 43.2 us  [shards(): pl.pallas_call(kernel, out_shape=pltpu.VMEM((4, 16, 256), F32), in_specs=...]
where the time goes in v7:
time: 44.2 us; the launch traced here: 43.9 us
  Pallas kernels  43.2 us (98%)
  local copies, waits for them, and re-layouts  0.66 us (1%)
    pallas_call x1, Pallas kernels, shards(): pl.pallas_call(kernel, out_shape=pltpu.VMEM((4, 16, 256), F32), in_specs=...  43.2 us

profile of v7, /device:TPU:16, one launch (start us, length us, event | category | flops | bytes accessed | tf_op | source)
XLA Modules:
  0.0 43.9 jit_solution(3396333384552046728)
XLA Ops:
  0.0 43.2 %shard_map.118 = f32[4,16,256]{2,1,0:T(8,128)S(1)} custom-call(bf16[64,2,128]{2,1,0:T(2,128)(2,1)} %bitcast.18, bf16[256,2,128]{2,1,0:T(2,128)(2,1)} %bitcast.17, f32[4,128,128]{2,1,0:T(8,128)} %cot_hbm.1, s32[4,64]{1,0:T(4,128)} %bitcast.19, bf16[4,64]{1,0:T(4,128)(2,1)} %bitcast.20, f32[1,64]{1,0:T(1,128)} %bitcast.22, s32[2,64]{1,0:T(2,128)} %bitcast.21, ...), custom_call_target="tpu_custom_call" | custom-call | tf_op jit(solution)/shard_map/pallas_call | solution.py:391
  43.2 0.7 %reshape.26 = f32[4,8,2,2,128]{4,3,2,1,0:T(2,128)} reshape(f32[4,16,256]{2,1,0:T(8,128)S(1)} %shard_map.118) | data formatting | bytes 131072 | tf_op jit(solution)/shard_map/reshape | solution.py:432

commit v8 on v7

--- a/solution.py
+++ b/solution.py
@@ -281,15 +281,15 @@
 
     def turn_z(t):
         total = send_z[t, pl.ds(pl.multiple_of(z * 16, 16), 16), :].astype(F32)
-        for d in range(1, NZ):
-            reduce_z(t, d).wait_recv()
-        for d in range(1, NZ):
-            total += recv_z[t, d - 1].astype(F32)
         if t == 3:
             for d in range(NZ):
                 reduce_far(d).wait_recv()
             for d in range(NZ):
                 total += recv_far[d].astype(F32)
+        for d in range(1, NZ):
+            reduce_z(t, d).wait_recv()
+        for d in range(1, NZ):
+            total += recv_z[t, d - 1].astype(F32)
         out[t] = total
 
     def sums(n, first, t):
@@ -301,6 +301,7 @@
         weights = et[:, pl.ds(pl.multiple_of(first * 8, 256), n * 8)]
         return [dot(weights, g) for g in grads]
 
+    acc[...] = jnp.zeros_like(acc)
     for d in range(1, NX):
         gather_x(0, d).wait_recv()
 
@@ -317,7 +318,6 @@
             acc[rows, :] = acc[rows, :] * k.astype(F32) + added[i]
         return carry
 
-    acc[...] = jnp.zeros_like(acc)
     lax.fori_loop(0, 2, first_tile, 0)
     send_x[0] = acc[...].astype(BF)
     for d in (2, 1, 3):

time: 44.2 us -> 44.1 us (level)
  no operation moved by 1% of the time
where the time goes in v8:
time: 44.1 us; the launch traced here: 43.8 us
  Pallas kernels  43.2 us (98%)
  local copies, waits for them, and re-layouts  0.66 us (1%)
    pallas_call x1, Pallas kernels, shards(): pl.pallas_call(kernel, out_shape=pltpu.VMEM((4, 16, 256), F32), in_specs=...  43.2 us

profile of v8, /device:TPU:16, one launch (start us, length us, event | category | flops | bytes accessed | tf_op | source)
XLA Modules:
  0.0 43.8 jit_solution(13333882735925486298)
XLA Ops:
  0.0 43.2 %shard_map.118 = f32[4,16,256]{2,1,0:T(8,128)S(1)} custom-call(bf16[64,2,128]{2,1,0:T(2,128)(2,1)} %bitcast.18, bf16[256,2,128]{2,1,0:T(2,128)(2,1)} %bitcast.17, f32[4,128,128]{2,1,0:T(8,128)} %cot_hbm.1, s32[4,64]{1,0:T(4,128)} %bitcast.19, bf16[4,64]{1,0:T(4,128)(2,1)} %bitcast.20, f32[1,64]{1,0:T(1,128)} %bitcast.22, s32[2,64]{1,0:T(2,128)} %bitcast.21, ...), custom_call_target="tpu_custom_call" | custom-call | tf_op jit(solution)/shard_map/pallas_call | solution.py:391
  43.2 0.7 %reshape.26 = f32[4,8,2,2,128]{4,3,2,1,0:T(2,128)} reshape(f32[4,16,256]{2,1,0:T(8,128)S(1)} %shard_map.118) | data formatting | bytes 131072 | tf_op jit(solution)/shard_map/reshape | solution.py:432
